TPU v7x, 512 devices: a whole 4x8x8 slice. The times are simulated.
512 devices in a mesh: dom: 128 (over y, z, core), rep: 4 (over x).
Axes of the slice: x: 4, y: 8, z: 8, core: 2. Of those that a mesh axis runs over, the one named last changes fastest.
Arguments:
- events: bfloat16 [4, 32768, 128], P('rep', 'dom'), may hold values from -6 to 6
- perm: int32 [4, 32768], P('rep', 'dom'), may hold values from 0 to 32767, as said below
- w_enc: bfloat16 [128, 256], replicated, may hold values from -0.5 to 0.5
- w_one: bfloat16 [256, 256], replicated, may hold values from -0.375 to 0.375
- w_two: bfloat16 [256, 256], replicated, may hold values from -0.375 to 0.375
- slot_blocks: int32 [4, 1280, 2], P('rep', 'dom'), may hold values from 0 to 255, as said below
- live_count: int32 [4, 128], P('rep', 'dom'), may hold values from 1 to 10, as said below
- block_counts: int32 [4, 1280, 128, 128], P('rep', 'dom'), may hold values from 0 to 3
- out_grad: bfloat16 [4, 32768, 256], P('rep', 'dom'), may hold values from -6 to 6
Outputs:
- embed: bfloat16 [4, 32768, 256], P('rep', 'dom')
- grad_enc: float32 [128, 256], replicated
- grad_one: float32 [256, 256], replicated
- grad_two: float32 [256, 256], replicated
Inputs may be any that keep to these rules, and one draw needn't show every extreme that they name: Within each batch perm names every account once, and the 256 time rows of each device hold exactly 256 // 128 accounts of each partition; account a belongs to partition a // 256. `slot_blocks`: slot s belongs to partition p = s // 10; its row block is one of p's 2 blocks; its column block is one of p's blocks, or the last block of partition p - 1, or the first block of partition p + 1, cyclically over partitions. Two slots may name the same pair; their counts add. `live_count`: in every batch some partition uses all 10 slots.
All inputs are finite; a program needn't handle non-finite values.
Results may differ from a plain program's by a relative error of at most 0.0075.
Values may be sent and summed in bfloat16 or wider, within the bound.
A program may use at most 64 MiB of HBM per device.

v0:
```python
import math

import jax
import jax.numpy as jnp
from jax import lax
from jax.sharding import PartitionSpec as P

loop_weight = 4.0


def with_halo(cells, sides, width):
    for axis, dim in sides:
        count = lax.axis_size(axis)
        head = lax.slice_in_dim(cells, 0, width, axis=dim)
        tail = lax.slice_in_dim(cells, cells.shape[dim] - width, cells.shape[dim], axis=dim)
        cells = jnp.concatenate(
            [
                lax.ppermute(tail, axis, [(i, (i + 1) % count) for i in range(count)]),
                cells,
                lax.ppermute(head, axis, [((i + 1) % count, i) for i in range(count)]),
            ],
            axis=dim,
        )
    return cells


def passed_along(block, axis, distance):
    devices = range(lax.axis_size(axis))
    route = [((i - distance) % len(devices), i) for i in devices]
    return lax.ppermute(block, axis, route)


def silu_slope(value):
    sig = jax.nn.sigmoid(value)
    return sig * (1.0 + value * (1.0 - sig))


def body(events, perm, w_enc, w_one, w_two, slot_blocks, live_count, block_counts, out_grad):
    rows_time = events[0]
    account_ids = perm[0]
    cotangent = out_grad[0]
    slot_pairs = slot_blocks[0]
    live_slots = live_count[0, 0]
    counts = block_counts[0]
    acc_dev = rows_time.shape[0]
    block = counts.shape[1]
    blk_dev = acc_dev // block
    hidden = w_one.shape[0]
    n_slots = counts.shape[0]
    dom_size = lax.axis_size("dom")
    rep_size = lax.axis_size("rep")
    partition = lax.axis_index("dom")
    scale_loss = 1.0 / math.sqrt(rep_size * dom_size * acc_dev)
    destination = account_ids // acc_dev
    ordering = jnp.argsort(destination, stable=True)
    sent_ids = account_ids[ordering]
    pre = jnp.dot(rows_time, w_enc, preferred_element_type=jnp.float32)
    encoded = jax.nn.silu(pre).astype(jnp.bfloat16)
    got_rows, got_ids = (
        lax.all_to_all(encoded[ordering], "dom", split_axis=0, concat_axis=0, tiled=True),
        lax.all_to_all(sent_ids, "dom", split_axis=0, concat_axis=0, tiled=True),
    )
    local_ids = got_ids - partition * acc_dev
    placing = jnp.argsort(local_ids)
    h_zero = got_rows[placing]
    row_local = slot_pairs[:, 0] - partition * blk_dev
    col_block = slot_pairs[:, 1]
    col_part = col_block // blk_dev
    prev_part = (partition - 1) % dom_size
    own_col = col_part == partition
    from_prev = (col_part == prev_part) & (col_block % blk_dev == blk_dev - 1)
    offsets = jnp.where(
        own_col,
        block + (col_block - partition * blk_dev) * block,
        jnp.where(from_prev, 0, block + acc_dev),
    )
    row_starts = row_local * block
    valid = jnp.arange(n_slots, dtype=jnp.int32) < live_slots
    row_onehot = (
        (row_local[:, None] == jnp.arange(blk_dev, dtype=jnp.int32)[None, :]) & valid[:, None]
    ).astype(jnp.float32)
    row_sums = jnp.sum(counts, axis=2).astype(jnp.float32)
    degree = loop_weight + jnp.dot(row_onehot.T, row_sums, precision=lax.Precision.HIGHEST).reshape(
        acc_dev
    )

    def propagate(field):
        window = with_halo(field, (("dom", 0),), block)

        def propagate_add_slot(slot_id, totals):
            adjacency = lax.dynamic_index_in_dim(counts, slot_id, 0, keepdims=False).astype(
                jnp.bfloat16
            )
            taken = lax.dynamic_slice_in_dim(window, offsets[slot_id], block, 0)
            product = jnp.dot(adjacency, taken, preferred_element_type=jnp.float32)
            current = lax.dynamic_slice_in_dim(totals, row_starts[slot_id], block, 0)
            return lax.dynamic_update_slice_in_dim(
                totals, current + product, row_starts[slot_id], 0
            )

        summed = lax.fori_loop(
            0, live_slots, propagate_add_slot, jnp.zeros((acc_dev, hidden), jnp.float32)
        )
        return (loop_weight * field.astype(jnp.float32) + summed) / degree[:, None]

    def transpose(field):

        def transpose_add_slot(slot_id, totals):
            adjacency = lax.dynamic_index_in_dim(counts, slot_id, 0, keepdims=False).astype(
                jnp.bfloat16
            )
            taken = lax.dynamic_slice_in_dim(field, row_starts[slot_id], block, 0)
            product = lax.dot_general(
                adjacency, taken, (((0,), (0,)), ((), ())), preferred_element_type=jnp.float32
            )
            current = lax.dynamic_slice_in_dim(totals, offsets[slot_id], block, 0)
            return lax.dynamic_update_slice_in_dim(totals, current + product, offsets[slot_id], 0)

        totals = lax.fori_loop(
            0, live_slots, transpose_add_slot, jnp.zeros((acc_dev + 2 * block, hidden), jnp.float32)
        )
        arrived = []
        for step_by, piece in ((1, totals[acc_dev + block :]), (-1, totals[:block])):
            arrived.append(passed_along(piece, "dom", step_by))
        owned = totals[block : block + acc_dev]
        owned = owned.at[:block].add(arrived[0])
        owned = owned.at[acc_dev - block :].add(arrived[1])
        return loop_weight * field.astype(jnp.float32) + owned

    z_one = jnp.dot(h_zero, w_one, preferred_element_type=jnp.float32).astype(jnp.bfloat16)
    agg_one = propagate(z_one)
    h_one = jax.nn.silu(agg_one).astype(jnp.bfloat16)
    z_two = jnp.dot(h_one, w_two, preferred_element_type=jnp.float32).astype(jnp.bfloat16)
    embed = propagate(z_two).astype(jnp.bfloat16)
    gs_two = (cotangent.astype(jnp.float32) * scale_loss / degree[:, None]).astype(jnp.bfloat16)
    gz_two = transpose(gs_two).astype(jnp.bfloat16)
    local_two = jnp.dot(h_one.T, gz_two, preferred_element_type=jnp.float32)
    gh_one = jnp.dot(gz_two, w_two.T, preferred_element_type=jnp.float32)
    gs_one = (gh_one * silu_slope(agg_one) / degree[:, None]).astype(jnp.bfloat16)
    gz_one = transpose(gs_one).astype(jnp.bfloat16)
    local_one = jnp.dot(h_zero.T, gz_one, preferred_element_type=jnp.float32)
    gh_zero = lax.optimization_barrier(
        jnp.dot(gz_one, w_one.T, preferred_element_type=jnp.float32).astype(jnp.bfloat16)
    )
    returned = lax.all_to_all(gh_zero[local_ids], "dom", split_axis=0, concat_axis=0, tiled=True)
    g_time = returned[jnp.argsort(ordering)]
    g_encoded = (g_time.astype(jnp.float32) * silu_slope(pre)).astype(jnp.bfloat16)
    local_enc = jnp.dot(rows_time.T, g_encoded, preferred_element_type=jnp.float32)
    grad_enc, grad_one, grad_two = lax.psum((local_enc, local_one, local_two), ("dom", "rep"))
    return (embed[None], grad_enc, grad_one, grad_two)


def solution(mesh):
    return jax.shard_map(
        body,
        mesh=mesh,
        in_specs=(
            P("rep", "dom", None),
            P("rep", "dom"),
            P(),
            P(),
            P(),
            P("rep", "dom", None),
            P("rep", "dom"),
            P("rep", "dom", None, None),
            P("rep", "dom", None),
        ),
        out_specs=(P("rep", "dom", None), P(), P(), P()),
        check_vma=False,
    )
```

profile of v0, /device:TPU:1, one launch (start us, length us, event | category | flops | bytes accessed | tf_op | source)
XLA Modules:
  0.0 686.7 jit_solution(6633529660277372230)
XLA Ops:
  7.9 3.2 sort.48
  11.1 1.9 gather_fusion.1
  13.8 18.6 %all-to-all-start.1 = ((s32[128,2,1]{1,2,0:T(1,128)}), s32[128,2,1]{1,2,0:T(1,128)S(1)}, u32[]{:S(2)}, u32[]{:S(2)}) async-start(s32[128,2,1]{1,2,0:T(1,128)} %bitcast.14), calls=%async_computation.1 | async-start | bytes 131072 | tf_op jit(solution)/shard_map/all_to_all | solution.py:61
  35.6 8.2 %all-to-all-done.1 = s32[128,2,1]{1,2,0:T(1,128)S(1)} async-done(((s32[128,2,1]{1,2,0:T(1,128)}), s32[128,2,1]{1,2,0:T(1,128)S(1)}, u32[]{:S(2)}, u32[]{:S(2)}) %all-to-all-start.1) | async-done | bytes 1056 | tf_op jit(solution)/shard_map/all_to_all | solution.py:61
  43.8 5.7 all-to-all-start
  51.1 3.2 sort.49
  54.2 7.6 %all-to-all-done = bf16[128,2,256]{2,1,0:T(2,128)(2,1)S(1)} async-done(((bf16[128,2,256]{2,1,0:T(2,128)(2,1)}), bf16[128,2,256]{2,1,0:T(2,128)(2,1)S(1)}, u32[]{:S(2)}, u32[]{:S(2)}) %all-to-all-start) | async-done | bytes 131104 | tf_op jit(solution)/shard_map/all_to_all | solution.py:60
  63.3 3.1 collective-permute-start
  66.4 1.9 collective-permute-start.1
  68.6 3.7 collective-permute-done.1
  72.4 7.5 %while.44 = (s32[]{:T(128)}, f32[256,256]{1,0:T(8,128)S(1)}, s32[]{:T(128)}, s32[10]{0:T(128)S(1)}, s32[10,128,128]{2,1,0:T(8,128)S(1)}, /*index=5*/s32[10]{0:T(...) while((s32[]{:T(128)}, f32[256,256]{1,0:T(8,128)S(1)}, ...), condition=%wide.region_3.4_spmd, body=%wide.region_2.3_spmd.sunk | while | flops 8437771 | bytes 655627 | solution.py:101
  80.3 62.0 %collective-permute-start.2 = (bf16[128,256]{1,0:T(8,128)(2,1)S(1)}, bf16[128,256]{1,0:T(8,128)(2,1)S(1)}, u32[]{:S(2)}, u32[]{:S(2)}) collective-permute-start(bf16[128,256]{1,0:T(8,128)(2,1)S(1)} %get-tuple-element.291), channel_id=1, source_target_pairs={{0,4},{4,8},{8,12},{12,16},{16,20},{20,24},{24,28},{28,32},{32,36}... | collective-permute-start | bytes 196616 | tf_op jit(solution)/shard_map/ppermute | solution.py:18
  142.3 5.9 collective-permute-start.3
  148.2 3.2 sort.50
  151.4 7.6 %while.45 = (s32[]{:T(128)}, f32[256,256]{1,0:T(8,128)S(1)}, s32[]{:T(128)}, s32[10]{0:T(128)S(1)}, s32[10,128,128]{2,1,0:T(8,128)S(1)}, /*index=5*/s32[10]{0:T(...) while((s32[]{:T(128)}, f32[256,256]{1,0:T(8,128)S(1)}, ...), condition=%wide.region_6.7_spmd, body=%wide.region_5.6_spmd.sunk | while | flops 8437771 | bytes 655627 | solution.py:101
  159.8 7.6 %while.46 = (s32[]{:T(128)}, f32[512,256]{1,0:T(8,128)S(1)}, s32[]{:T(128)}, s32[10]{0:T(128)S(1)}, s32[10,128,128]{2,1,0:T(8,128)S(1)}, /*index=5*/s32[10]{0:T(...) while((s32[]{:T(128)}, f32[512,256]{1,0:T(8,128)S(1)}, ...), condition=%wide.region_8.9_spmd, body=%wide.region_7.8_spmd.sunk | while | flops 8437771 | bytes 655627 | solution.py:119
  167.4 120.9 %collective-permute-start.4 = (f32[128,256]{1,0:T(8,128)S(1)}, f32[128,256]{1,0:T(8,128)S(1)}, u32[]{:S(2)}, u32[]{:S(2)}) collective-permute-start(f32[128,256]{1,0:T(8,128)S(1)} %get-tuple-element.290), channel_id=1, source_target_pairs={{508,0},{0,4},{4,8},{8,12},{12,16},{16,20},{20,24},{24,28},{28,32}... | collective-permute-start | bytes 393224 | tf_op jit(solution)/shard_map/ppermute | solution.py:30
  288.5 11.6 %collective-permute-start.5 = (f32[128,256]{1,0:T(8,128)S(1)}, f32[128,256]{1,0:T(8,128)S(1)}, u32[]{:S(2)}, u32[]{:S(2)}) collective-permute-start(f32[128,256]{1,0:T(8,128)S(1)} %get-tuple-element.289), channel_id=1, source_target_pairs={{4,0},{8,4},{12,8},{16,12},{20,16},{24,20},{28,24},{32,28},{36,32}... | collective-permute-start | bytes 393224 | tf_op jit(solution)/shard_map/ppermute | solution.py:30
  301.4 7.6 %while.47 = (s32[]{:T(128)}, f32[512,256]{1,0:T(8,128)S(1)}, s32[]{:T(128)}, s32[10]{0:T(128)S(1)}, s32[10,128,128]{2,1,0:T(8,128)S(1)}, /*index=5*/s32[10]{0:T(...) while((s32[]{:T(128)}, f32[512,256]{1,0:T(8,128)S(1)}, ...), condition=%wide.region_10.11_spmd, body=%wide.region_9.10_spmd.sunk | while | flops 8437771 | bytes 655627 | solution.py:119
  309.0 56.3 %collective-permute-start.6 = (f32[128,256]{1,0:T(8,128)S(1)}, f32[128,256]{1,0:T(8,128)S(1)}, u32[]{:S(2)}, u32[]{:S(2)}) collective-permute-start(f32[128,256]{1,0:T(8,128)S(1)} %get-tuple-element.288), channel_id=1, source_target_pairs={{508,0},{0,4},{4,8},{8,12},{12,16},{16,20},{20,24},{24,28},{28,32}... | collective-permute-start | bytes 393224 | tf_op jit(solution)/shard_map/ppermute | solution.py:30
  365.3 16.6 %collective-permute-start.7 = (f32[128,256]{1,0:T(8,128)S(1)}, f32[128,256]{1,0:T(8,128)S(1)}, u32[]{:S(2)}, u32[]{:S(2)}) collective-permute-start(f32[128,256]{1,0:T(8,128)S(1)} %get-tuple-element.287), channel_id=1, source_target_pairs={{4,0},{8,4},{12,8},{16,12},{20,16},{24,20},{28,24},{32,28},{36,32}... | collective-permute-start | bytes 393224 | tf_op jit(solution)/shard_map/ppermute | solution.py:30
  385.0 14.4 %all-to-all-start.2 = ((bf16[128,2,256]{2,1,0:T(2,128)(2,1)}), bf16[128,2,256]{2,1,0:T(2,128)(2,1)S(1)}, u32[]{:S(2)}, u32[]{:S(2)}) async-start(bf16[128,2,256]{2,1,0:T(2,128)(2,1)} %all_to_all.27), calls=%async_computation.2 | async-start | bytes 262144 | tf_op jit(solution)/shard_map/all_to_all | solution.py:145
  401.3 10.3 %all-to-all-done.2 = bf16[128,2,256]{2,1,0:T(2,128)(2,1)S(1)} async-done(((bf16[128,2,256]{2,1,0:T(2,128)(2,1)}), bf16[128,2,256]{2,1,0:T(2,128)(2,1)S(1)}, u32[]{:S(2)}, u32[]{:S(2)}) %all-to-all-start.2) | async-done | bytes 131104 | tf_op jit(solution)/shard_map/all_to_all | solution.py:145
  413.8 262.6 %all-reduce.3.cloned.1.call-done = (f32[128,256]{0,1:T(8,128)}, f32[256,256]{1,0:T(8,128)}, f32[256,256]{1,0:T(8,128)}) async-done(((f32[128,256]{0,1:T(8,128)}, f32[256,256]{1,0:T(8,128)}, f32[256,256]{1,0:T(8,128)}), (f32[128,256]{0,1:T(8,128)}, f32[256,256]{1,0:T(8,128)}, f32[256,256]{1,0:T(8,128)})) %all-reduce.3.cloned.1.call-update) | async-done | bytes 655376 | tf_op jit(solution)/shard_map/psum | solution.py:149
  (104 shorter events, 29.9 us)
Async XLA Ops:
  7.2 72.9 %copy-start = (bf16[256,256]{1,0:T(8,128)(2,1)S(1)}, bf16[256,256]{1,0:T(8,128)(2,1)}, u32[]{:S(2)}) copy-start(bf16[256,256]{1,0:T(8,128)(2,1)} %param.29) | copy-start | bytes 393220
  7.2 0.7 copy-start.1
  13.8 19.3 %copy-start.7 = (s32[1,10,2]{1,2,0:T(2,128)S(1)}, s32[1,10,2]{1,2,0:T(2,128)}, u32[]{:S(2)}) copy-start(s32[1,10,2]{1,2,0:T(2,128)} %param.30) | copy-start | bytes 244
  13.8 19.4 %copy-start.8 = (bf16[128,256]{1,0:T(8,128)(2,1)S(1)}, bf16[128,256]{1,0:T(8,128)(2,1)}, u32[]{:S(2)}) copy-start(bf16[128,256]{1,0:T(8,128)(2,1)} %param.27) | copy-start | bytes 196612
  13.8 19.4 %copy-start.9 = (bf16[1,256,128]{2,1,0:T(8,128)(2,1)S(1)}, bf16[1,256,128]{2,1,0:T(8,128)(2,1)}, u32[]{:S(2)}) copy-start(bf16[1,256,128]{2,1,0:T(8,128)(2,1)} %param.25) | copy-start | bytes 196612
  13.8 30.0 %all-to-all-start.1 = ((s32[128,2,1]{1,2,0:T(1,128)}), s32[128,2,1]{1,2,0:T(1,128)S(1)}, u32[]{:S(2)}, u32[]{:S(2)}) async-start(s32[128,2,1]{1,2,0:T(1,128)} %bitcast.14), calls=%async_computation.1 | async-start | bytes 131072 | tf_op jit(solution)/shard_map/all_to_all | solution.py:61
  32.4 1.1 copy-start.2
  43.8 18.0 %all-to-all-start = ((bf16[128,2,256]{2,1,0:T(2,128)(2,1)}), bf16[128,2,256]{2,1,0:T(2,128)(2,1)S(1)}, u32[]{:S(2)}, u32[]{:S(2)}) async-start(bf16[128,2,256]{2,1,0:T(2,128)(2,1)} %all_to_all.22), calls=%async_computation | async-start | bytes 262144 | tf_op jit(solution)/shard_map/all_to_all | solution.py:60
  61.9 1.2 copy-start.3
  63.3 5.3 collective-permute-start
  66.4 5.9 collective-permute-start.1
  80.3 71.0 %collective-permute-start.2 = (bf16[128,256]{1,0:T(8,128)(2,1)S(1)}, bf16[128,256]{1,0:T(8,128)(2,1)S(1)}, u32[]{:S(2)}, u32[]{:S(2)}) collective-permute-start(bf16[128,256]{1,0:T(8,128)(2,1)S(1)} %get-tuple-element.291), channel_id=1, source_target_pairs={{0,4},{4,8},{8,12},{12,16},{16,20},{20,24},{24,28},{28,32},{32,36}... | collective-permute-start | bytes 196616 | tf_op jit(solution)/shard_map/ppermute | solution.py:18
  142.3 9.1 %collective-permute-start.3 = (bf16[128,256]{1,0:T(8,128)(2,1)S(1)}, bf16[128,256]{1,0:T(8,128)(2,1)S(1)}, u32[]{:S(2)}, u32[]{:S(2)}) collective-permute-start(bf16[128,256]{1,0:T(8,128)(2,1)S(1)} %get-tuple-element.292), channel_id=1, source_target_pairs={{4,0},{8,4},{12,8},{16,12},{20,16},{24,20},{28,24},{32,28},{36,32}... | collective-permute-start | bytes 196616 | tf_op jit(solution)/shard_map/ppermute | solution.py:20
  151.4 7.6 %copy-start.6 = (bf16[1,256,256]{2,1,0:T(8,128)(2,1)S(1)}, bf16[1,256,256]{2,1,0:T(8,128)(2,1)}, u32[]{:S(2)}) copy-start(bf16[1,256,256]{2,1,0:T(8,128)(2,1)} %param.33) | copy-start | bytes 393220
  167.4 132.7 %collective-permute-start.4 = (f32[128,256]{1,0:T(8,128)S(1)}, f32[128,256]{1,0:T(8,128)S(1)}, u32[]{:S(2)}, u32[]{:S(2)}) collective-permute-start(f32[128,256]{1,0:T(8,128)S(1)} %get-tuple-element.290), channel_id=1, source_target_pairs={{508,0},{0,4},{4,8},{8,12},{12,16},{16,20},{20,24},{24,28},{28,32}... | collective-permute-start | bytes 393224 | tf_op jit(solution)/shard_map/ppermute | solution.py:30
  288.5 12.6 %collective-permute-start.5 = (f32[128,256]{1,0:T(8,128)S(1)}, f32[128,256]{1,0:T(8,128)S(1)}, u32[]{:S(2)}, u32[]{:S(2)}) collective-permute-start(f32[128,256]{1,0:T(8,128)S(1)} %get-tuple-element.289), channel_id=1, source_target_pairs={{4,0},{8,4},{12,8},{16,12},{20,16},{24,20},{28,24},{32,28},{36,32}... | collective-permute-start | bytes 393224 | tf_op jit(solution)/shard_map/ppermute | solution.py:30
  309.0 72.9 %collective-permute-start.6 = (f32[128,256]{1,0:T(8,128)S(1)}, f32[128,256]{1,0:T(8,128)S(1)}, u32[]{:S(2)}, u32[]{:S(2)}) collective-permute-start(f32[128,256]{1,0:T(8,128)S(1)} %get-tuple-element.288), channel_id=1, source_target_pairs={{508,0},{0,4},{4,8},{8,12},{12,16},{16,20},{20,24},{24,28},{28,32}... | collective-permute-start | bytes 393224 | tf_op jit(solution)/shard_map/ppermute | solution.py:30
  365.3 17.5 %collective-permute-start.7 = (f32[128,256]{1,0:T(8,128)S(1)}, f32[128,256]{1,0:T(8,128)S(1)}, u32[]{:S(2)}, u32[]{:S(2)}) collective-permute-start(f32[128,256]{1,0:T(8,128)S(1)} %get-tuple-element.287), channel_id=1, source_target_pairs={{4,0},{8,4},{12,8},{16,12},{20,16},{24,20},{28,24},{32,28},{36,32}... | collective-permute-start | bytes 393224 | tf_op jit(solution)/shard_map/ppermute | solution.py:30
  385.0 26.6 %all-to-all-start.2 = ((bf16[128,2,256]{2,1,0:T(2,128)(2,1)}), bf16[128,2,256]{2,1,0:T(2,128)(2,1)S(1)}, u32[]{:S(2)}, u32[]{:S(2)}) async-start(bf16[128,2,256]{2,1,0:T(2,128)(2,1)} %all_to_all.27), calls=%async_computation.2 | async-start | bytes 262144 | tf_op jit(solution)/shard_map/all_to_all | solution.py:145
  399.4 277.0 %all-reduce.3.cloned.1.call-start = ((), (), s32[]{:S(2)}) async-start(), calls=%async_computation.3 | async-start | bytes 1310720 | tf_op jit(solution)/shard_map/psum | solution.py:149
  676.4 1.7 copy-start.5
  678.1 1.0 copy-start.4
Sparse Core Ops, SparseCore 0:
  413.9 262.4 all-reduce.2
where the time goes:
time: 691 us; the launch traced here: 687 us
  starting transfers between devices  317 us (46%)
  waiting for transfers between devices  294 us (43%)
  local copies, waits for them, and re-layouts  22.8 us (3%)
  loops' own time  20.9 us (3%)
  between operations  15.3 us (2%)
  other arithmetic  11.7 us (2%)
    psum x1, waiting for transfers between devices, body(): lax.psum((local_enc, local_one, local_two), ('dom', 'rep'))  263 us
    ppermute x4, starting transfers between devices, passed_along(): return lax.ppermute(block, axis, route)  205 us
    ppermute x2, starting transfers between devices, with_halo(): lax.ppermute(tail, axis, [(i, (i + 1) % count) for i in range(count)])  65.1 us
    all_to_all x1, starting transfers between devices, body(): lax.all_to_all(sent_ids, 'dom', split_axis=0, concat_axis=0, tiled=True)  18.6 us
    all_to_all x1, starting transfers between devices, body(): lax.all_to_all(gh_zero[local_ids], 'dom', split_axis=0, concat_axis=0, ti...  14.4 us
  transfers between devices with their start and end apart: 12, of which 7 were waited for; matrix products, arithmetic and copies ran while one was open for 2% of the time, Pallas kernels for 0%

commit v1 on v0

v1 whole, which is shorter than its diff:
```python
import functools
import math

import jax
import jax.numpy as jnp
from jax import lax
from jax.experimental import pallas as pl
from jax.experimental.pallas import tpu as pltpu
from jax.sharding import PartitionSpec as P

loop_weight = 4.0
NY = 8
NZ = 16
NX = 4
F32 = jnp.float32
BF16 = jnp.bfloat16


def dot(a, b):
    return jnp.dot(a, b, preferred_element_type=F32)


def dot_nt(a, b):
    return lax.dot_general(a, b, (((1,), (1,)), ((), ())), preferred_element_type=F32)


def dot_tn(a, b):
    return lax.dot_general(a, b, (((0,), (0,)), ((), ())), preferred_element_type=F32)


def sigmoid(value):
    return 1.0 / (1.0 + jnp.exp(-value))


def wait_for(ref, sem):
    pltpu.make_async_copy(ref, ref, sem).wait()


def step_kernel(
    scale_loss,
    events, perm, w_enc, w_one, w_two, slots, live, counts, out_grad,
    embed, grad_enc, grad_one, grad_two,
    adj_f, adj, adj_t, inv_deg, mid, ev_win, z_one, z_two, gs_ref, gz_ref, gh_ref,
    a_src, a_dst, b_src, b_dst, qa_src, qa_dst, qb_src, qb_dst,
    rs_src, rs_dst, y_dst, x_dst, ag_dst,
    send_sem, recv_sem,
):
    me = lax.axis_index("dom")
    rep = lax.axis_index("rep")
    ndom = NY * NZ
    my_y = me // NZ
    my_z = me % NZ
    left = (me + ndom - 1) % ndom
    right = (me + 1) % ndom

    def in_y(j):
        return (my_y + j) % NY

    def in_z(j):
        return (my_z + j) % NZ

    def in_x(j):
        return (rep + j) % NX

    barrier = pltpu.get_barrier_semaphore()

    def hello(device):
        pl.semaphore_signal(barrier, inc=1, device_id=device, device_id_type=pl.DeviceIdType.MESH)

    for j in range(1, NY):
        hello({"dom": in_y(j) * NZ + my_z})
    for j in range(1, NZ):
        hello({"dom": my_y * NZ + in_z(j)})
    for j in range(1, NX):
        hello({"rep": in_x(j)})
    hello({"dom": left})
    hello({"dom": right})

    def send(src, dst, step, device):
        pltpu.make_async_remote_copy(
            src_ref=src, dst_ref=dst, send_sem=send_sem.at[step], recv_sem=recv_sem.at[step],
            device_id=device, device_id_type=pl.DeviceIdType.MESH,
        ).start()

    rows = lax.broadcasted_iota(jnp.int32, (256, 256), 0)
    cols = lax.broadcasted_iota(jnp.int32, (256, 256), 1)
    ids = perm[...]
    ids_row = ids.astype(F32)
    ids_col = jnp.sum(jnp.where(rows == cols, ids_row, 0.0), axis=1, keepdims=True)
    place = jnp.sum(jnp.where(ids_col < ids_row, 1.0, 0.0), axis=0, keepdims=True)
    sorting = jnp.where(rows.astype(F32) == place, 1.0, 0.0).astype(BF16)
    local_col = (ids_col.astype(jnp.int32) & 255).astype(F32)
    local_rep = jnp.broadcast_to(local_col, (256, 128)).astype(BF16)
    a_src[:, :, 0:128] = dot(sorting, events[0]).astype(BF16).reshape(NY, 32, 128)
    a_src[:, :, 128:256] = dot(sorting, local_rep).astype(BF16).reshape(NY, 32, 128)

    pl.semaphore_wait(barrier, NY - 1 + NZ - 1 + NX - 1 + 2)

    for j in range(1, NY):
        to = in_y(j)
        send(a_src.at[to], a_dst.at[my_y], 0, {"dom": to * NZ + my_z})
    a_dst[my_y] = a_src[my_y]

    weights = []
    for s in range(10):
        row = slots[0, s, 0] - 2 * me
        col = (slots[0, s, 1] - 2 * me + 1 + 2 * ndom) % (2 * ndom)
        used = s < live[0, 0]
        weights.append(
            [[jnp.where(used & (row == r) & (col == c), 1.0, 0.0) for c in range(4)] for r in range(2)]
        )
    for part in range(4):
        here = slice(part * 32, part * 32 + 32)
        sums = [[None] * 4 for _ in range(2)]
        for s in range(10):
            cell = counts[0, s, here, :].astype(F32)
            for r in range(2):
                for c in range(4):
                    term = cell * weights[s][r][c]
                    sums[r][c] = term if s == 0 else sums[r][c] + term
        diag = (
            lax.broadcasted_iota(jnp.int32, (32, 128), 0) + part * 32
            == lax.broadcasted_iota(jnp.int32, (32, 128), 1)
        )
        for r in range(2):
            sums[r][r + 1] = sums[r][r + 1] + jnp.where(diag, loop_weight, 0.0)
            for c in range(4):
                adj_f[r * 128 + part * 32 : r * 128 + part * 32 + 32, c * 128 : c * 128 + 128] = sums[r][c]
    adj[...] = adj_f[...].astype(BF16)
    for r in range(2):
        for c in range(4):
            adj_t[c * 128 : c * 128 + 128, r * 128 : r * 128 + 128] = (
                adj_f[r * 128 : r * 128 + 128, c * 128 : c * 128 + 128].T.astype(BF16)
            )
    inverse = 1.0 / dot(adj[...], jnp.ones((512, 128), BF16))
    inv_deg[:, 0:128] = inverse
    inv_deg[:, 128:256] = inverse

    gs_two = (out_grad[0].astype(F32) * scale_loss * inv_deg[...]).astype(BF16)
    qa_src[0] = dot(adj_t[0:128], gs_two).astype(BF16)
    qa_src[1] = dot(adj_t[384:512], gs_two).astype(BF16)
    send(qa_src.at[0], qa_dst.at[1], 1, {"dom": left})
    send(qa_src.at[1], qa_dst.at[0], 2, {"dom": right})
    gz_ref[...] = dot(adj_t[128:384], gs_two)

    source = ((rows >> 1) & (NY - 1)) * 32 + (rows >> 4) * 2 + (rows & 1)
    mid[...] = jnp.where(cols == source, 1.0, 0.0).astype(BF16)

    wait_for(a_dst.at[pl.ds(0, NY - 1)], recv_sem.at[0])
    b_src[...] = dot(mid[...], a_dst[...].reshape(256, 256)).astype(BF16).reshape(NZ, 16, 256)
    for j in range(1, NZ):
        to = in_z(j)
        send(b_src.at[to], b_dst.at[my_z], 3, {"dom": my_y * NZ + to})
    b_dst[my_z] = b_src[my_z]

    wait_for(qa_dst.at[1], recv_sem.at[1])
    wait_for(qa_dst.at[0], recv_sem.at[2])
    gz_two = (gz_ref[...] + qa_dst[...].astype(F32).reshape(256, 256)).astype(BF16)
    gh_ref[...] = dot_nt(gz_two, w_two[...]) * inv_deg[...]

    wait_for(b_dst.at[pl.ds(0, NZ - 1)], recv_sem.at[3])
    got = b_dst[...].reshape(256, 256)
    got_ids = got[:, 128:256].astype(F32)
    lane = cols[:, 0:128].astype(F32)
    placing = jnp.concatenate(
        [jnp.where(got_ids == lane, 1.0, 0.0), jnp.where(got_ids == lane + 128.0, 1.0, 0.0)], axis=1
    ).astype(BF16)
    ev_win[128:384] = dot_tn(placing, got[:, 0:128]).astype(BF16)
    send(ev_win.at[pl.ds(128, 128)], ev_win.at[pl.ds(384, 128)], 4, {"dom": left})
    send(ev_win.at[pl.ds(256, 128)], ev_win.at[pl.ds(0, 128)], 5, {"dom": right})

    def encoded(rows_in):
        pre_rows = dot(rows_in, w_enc[...])
        return pre_rows, (pre_rows * sigmoid(pre_rows)).astype(BF16)

    ev_own = ev_win[128:384]
    pre, h_zero = encoded(ev_own)
    z_own = dot(h_zero, w_one[...]).astype(BF16)
    total = dot(adj[:, 128:384], z_own)
    wait_for(ev_win.at[pl.ds(384, 128)], recv_sem.at[4])
    wait_for(ev_win.at[pl.ds(0, 128)], recv_sem.at[5])
    for where in (0, 384):
        z_side = dot(encoded(ev_win[where : where + 128])[1], w_one[...]).astype(BF16)
        total = total + dot(adj[:, where : where + 128], z_side)
    agg_one = total * inv_deg[...]
    sig = sigmoid(agg_one)
    h_one = (agg_one * sig).astype(BF16)
    z_two[128:384] = dot(h_one, w_two[...]).astype(BF16)
    send(z_two.at[pl.ds(128, 128)], z_two.at[pl.ds(384, 128)], 6, {"dom": left})
    send(z_two.at[pl.ds(256, 128)], z_two.at[pl.ds(0, 128)], 7, {"dom": right})
    gs_one = (gh_ref[...] * (sig * (1.0 + agg_one * (1.0 - sig)))).astype(BF16)
    qb_src[0] = dot(adj_t[0:128], gs_one).astype(BF16)
    qb_src[1] = dot(adj_t[384:512], gs_one).astype(BF16)
    send(qb_src.at[0], qb_dst.at[1], 8, {"dom": left})
    send(qb_src.at[1], qb_dst.at[0], 9, {"dom": right})
    gz_own = dot(adj_t[128:384], gs_one)
    rs_src[:, :, 0:256] = dot_tn(h_one, gz_two).astype(BF16).reshape(NZ, 16, 256)

    wait_for(qb_dst.at[1], recv_sem.at[8])
    wait_for(qb_dst.at[0], recv_sem.at[9])
    gz_one = (gz_own + qb_dst[...].astype(F32).reshape(256, 256)).astype(BF16)
    rs_src[:, :, 256:512] = dot_tn(h_zero, gz_one).astype(BF16).reshape(NZ, 16, 256)
    gh_zero = dot_nt(gz_one, w_one[...]).astype(BF16)
    sig = sigmoid(pre)
    g_enc = (gh_zero.astype(F32) * (sig * (1.0 + pre * (1.0 - sig)))).astype(BF16)
    l_enc = dot_tn(ev_own, g_enc).astype(BF16)
    for k in range(NZ):
        r, c = 16 * (k // 2), 128 * (k % 2)
        rs_src[k, :, 512:640] = l_enc[r : r + 16, c : c + 128]

    for j in range(1, NZ):
        to = in_z(j)
        send(rs_src.at[to], rs_dst.at[my_z], 10, {"dom": my_y * NZ + to})
    rs_dst[my_z] = rs_src[my_z]

    wait_for(z_two.at[pl.ds(384, 128)], recv_sem.at[6])
    wait_for(z_two.at[pl.ds(0, 128)], recv_sem.at[7])
    embed[0] = (dot(adj[...], z_two[...]) * inv_deg[...]).astype(BF16)

    wait_for(rs_dst.at[pl.ds(0, NZ - 1)], recv_sem.at[10])
    y_dst[my_y] = jnp.sum(rs_dst[...].astype(F32), axis=0).astype(BF16)
    for j in range(1, NY):
        send(y_dst.at[my_y], y_dst.at[my_y], 11, {"dom": in_y(j) * NZ + my_z})
    wait_for(y_dst.at[pl.ds(0, NY - 1)], recv_sem.at[11])
    x_dst[rep] = jnp.sum(y_dst[...].astype(F32), axis=0).astype(BF16)
    for j in range(1, NX):
        send(x_dst.at[rep], x_dst.at[rep], 12, {"rep": in_x(j)})
    wait_for(x_dst.at[pl.ds(0, NX - 1)], recv_sem.at[12])
    ag_dst[my_z] = jnp.sum(x_dst[...].astype(F32), axis=0).astype(BF16)
    for j in range(1, NZ):
        send(ag_dst.at[my_z], ag_dst.at[my_z], 13, {"dom": my_y * NZ + in_z(j)})
    wait_for(ag_dst.at[pl.ds(0, NZ - 1)], recv_sem.at[13])
    grad_two[...] = ag_dst[:, :, 0:256].astype(F32).reshape(256, 256)
    grad_one[...] = ag_dst[:, :, 256:512].astype(F32).reshape(256, 256)
    for k in range(NZ):
        r, c = 16 * (k // 2), 128 * (k % 2)
        grad_enc[r : r + 16, c : c + 128] = ag_dst[k, :, 512:640].astype(F32)

    wait_for(a_src.at[pl.ds(0, NY - 1)], send_sem.at[0])
    wait_for(qa_src.at[0], send_sem.at[1])
    wait_for(qa_src.at[1], send_sem.at[2])
    wait_for(b_src.at[pl.ds(0, NZ - 1)], send_sem.at[3])
    for step, ref in ((4, ev_win), (5, ev_win), (6, z_two), (7, z_two)):
        wait_for(ref.at[pl.ds(0, 128)], send_sem.at[step])
    wait_for(qb_src.at[0], send_sem.at[8])
    wait_for(qb_src.at[1], send_sem.at[9])
    wait_for(rs_src.at[pl.ds(0, NZ - 1)], send_sem.at[10])
    wait_for(y_dst.at[pl.ds(0, NY - 1)], send_sem.at[11])
    wait_for(x_dst.at[pl.ds(0, NX - 1)], send_sem.at[12])
    wait_for(ag_dst.at[pl.ds(0, NZ - 1)], send_sem.at[13])


def body(events, perm, w_enc, w_one, w_two, slot_blocks, live_count, block_counts, out_grad):
    scale_loss = 1.0 / math.sqrt(lax.axis_size("rep") * lax.axis_size("dom") * events.shape[1])
    vmem = pl.BlockSpec(memory_space=pltpu.VMEM)
    smem = pl.BlockSpec(memory_space=pltpu.SMEM)
    return pl.pallas_call(
        functools.partial(step_kernel, scale_loss),
        out_shape=(
            jax.ShapeDtypeStruct((1, 256, 256), BF16),
            jax.ShapeDtypeStruct((128, 256), F32),
            jax.ShapeDtypeStruct((256, 256), F32),
            jax.ShapeDtypeStruct((256, 256), F32),
        ),
        in_specs=[vmem, vmem, vmem, vmem, vmem, smem, smem, vmem, vmem],
        out_specs=(vmem, vmem, vmem, vmem),
        scratch_shapes=[
            pltpu.VMEM((256, 512), F32),
            pltpu.VMEM((256, 512), BF16),
            pltpu.VMEM((512, 256), BF16),
            pltpu.VMEM((256, 256), F32),
            pltpu.VMEM((256, 256), BF16),
            pltpu.VMEM((512, 128), BF16),
            pltpu.VMEM((512, 256), BF16),
            pltpu.VMEM((512, 256), BF16),
            pltpu.VMEM((256, 256), BF16),
            pltpu.VMEM((256, 256), F32),
            pltpu.VMEM((256, 256), F32),
            pltpu.VMEM((NY, 32, 256), BF16),
            pltpu.VMEM((NY, 32, 256), BF16),
            pltpu.VMEM((NZ, 16, 256), BF16),
            pltpu.VMEM((NZ, 16, 256), BF16),
            pltpu.VMEM((2, 128, 256), BF16),
            pltpu.VMEM((2, 128, 256), BF16),
            pltpu.VMEM((2, 128, 256), BF16),
            pltpu.VMEM((2, 128, 256), BF16),
            pltpu.VMEM((NZ, 16, 640), BF16),
            pltpu.VMEM((NZ, 16, 640), BF16),
            pltpu.VMEM((NY, 16, 640), BF16),
            pltpu.VMEM((NX, 16, 640), BF16),
            pltpu.VMEM((NZ, 16, 640), BF16),
            pltpu.SemaphoreType.DMA((14,)),
            pltpu.SemaphoreType.DMA((14,)),
        ],
        compiler_params=pltpu.CompilerParams(
            collective_id=0, has_side_effects=True, vmem_limit_bytes=32 * 1024 * 1024
        ),
    )(events, perm, w_enc, w_one, w_two, slot_blocks, live_count, block_counts, out_grad)


def solution(mesh):
    return jax.shard_map(
        body,
        mesh=mesh,
        in_specs=(
            P("rep", "dom", None),
            P("rep", "dom"),
            P(),
            P(),
            P(),
            P("rep", "dom", None),
            P("rep", "dom"),
            P("rep", "dom", None, None),
            P("rep", "dom", None),
        ),
        out_specs=(P("rep", "dom", None), P(), P(), P()),
        check_vma=False,
    )
```

time: 691 us -> 76.8 us (0.11)
  starting transfers between devices: 317 us -> 0 us
  waiting for transfers between devices: 294 us -> 0 us
  Pallas kernels: 0 us -> 66.3 us
  loops' own time: 20.9 us -> 0 us
  between operations: 15.3 us -> 1.32 us
  local copies, waits for them, and re-layouts: 22.8 us -> 8.88 us
  other arithmetic: 11.7 us -> 0 us
    ppermute x8 -> x0, starting transfers between devices: 278 us -> none  [the longest x4 205 us: passed_along(): return lax.ppermute(block, axis, route)]
    psum x1 -> x0, waiting for transfers between devices: 263 us -> none  [body(): lax.psum((local_enc, local_one, local_two), ('dom', 'rep'))]
    pallas_call x0 -> x1, Pallas kernels: none -> 66.3 us  [body(): pl.pallas_call(functools.partial(step_kernel, scale_loss), out_shape=(jax...]
    all_to_all x3 -> x0, starting transfers between devices: 38.7 us -> none  [the longest x1 18.6 us: body(): lax.all_to_all(sent_ids, 'dom', split_axis=0, concat_axis=0, tiled=True)]
    all_to_all x3 -> x0, waiting for transfers between devices: 26.1 us -> none  [the longest x1 10.3 us: body(): lax.all_to_all(gh_zero[local_ids], 'dom', split_axis=0, concat_axis=0, ti...]
    another operation x4 -> x0, loops' own time: 20.9 us -> none  [the longest x2 10.5 us: propagate(): lax.fori_loop(0, live_slots, propagate_add_slot, jnp.zeros((acc_dev, hidd...]
    sort x3 -> x0, other arithmetic: 9.5 us -> none  [the longest x1 3.17 us: body(): ordering = jnp.argsort(destination, stable=True)]
  transfers between devices with their start and end apart: 12 -> 0, of which waited for: 7 -> 0; matrix products, arithmetic and copies ran while one was open for 2% -> 0% of each run, Pallas kernels for 0% -> 0%
where the time goes in v1:
time: 76.8 us; the launch traced here: 76.5 us
  Pallas kernels  66.3 us (86%)
  local copies, waits for them, and re-layouts  8.88 us (12%)
  between operations  1.32 us (2%)
    pallas_call x1, Pallas kernels, body(): pl.pallas_call(functools.partial(step_kernel, scale_loss), out_shape=(jax...  66.3 us
    unnamed x21, local copies, waits for them, and re-layouts  8.88 us

profile of v1, /device:TPU:1, one launch (start us, length us, event | category | flops | bytes accessed | tf_op | source)
XLA Modules:
  0.0 76.5 jit_solution(13581696667540631829)
XLA Ops:
  0.6 0.0 copy-start.7
  1.3 0.0 copy-done.7
  1.3 0.0 copy-start.6
  1.3 0.1 copy.13.slots
  1.4 0.6 copy-done.6
  2.0 0.0 copy-start
  2.0 1.1 %copy-done = s32[1,10,128,128]{3,2,1,0:T(8,128)S(1)} copy-done((s32[1,10,128,128]{3,2,1,0:T(8,128)S(1)}, s32[1,10,128,128]{3,2,1,0:T(8,128)}, u32[]{:S(2)}) %copy-start) | copy-done | bytes 655384
  3.1 0.0 copy-start.1
  3.1 0.9 %copy-done.1 = bf16[256,256]{1,0:T(8,128)(2,1)S(1)} copy-done((bf16[256,256]{1,0:T(8,128)(2,1)S(1)}, bf16[256,256]{1,0:T(8,128)(2,1)}, u32[]{:S(2)}) %copy-start.1) | copy-done | bytes 131096
  4.0 0.0 copy-start.2
  4.0 0.9 %copy-done.2 = bf16[256,256]{1,0:T(8,128)(2,1)S(1)} copy-done((bf16[256,256]{1,0:T(8,128)(2,1)S(1)}, bf16[256,256]{1,0:T(8,128)(2,1)}, u32[]{:S(2)}) %copy-start.2) | copy-done | bytes 131096
  4.9 0.0 copy-start.3
  4.9 0.9 %copy-done.3 = bf16[1,256,256]{2,1,0:T(8,128)(2,1)S(1)} copy-done((bf16[1,256,256]{2,1,0:T(8,128)(2,1)S(1)}, bf16[1,256,256]{2,1,0:T(8,128)(2,1)}, u32[]{:S(2)}) %copy-start.3) | copy-done | bytes 131096
  5.8 0.0 copy-start.4
  5.8 0.8 %copy-done.4 = bf16[1,256,128]{2,1,0:T(8,128)(2,1)S(1)} copy-done((bf16[1,256,128]{2,1,0:T(8,128)(2,1)S(1)}, bf16[1,256,128]{2,1,0:T(8,128)(2,1)}, u32[]{:S(2)}) %copy-start.4) | copy-done | bytes 65560
  6.6 0.0 copy-start.5
  6.6 0.8 %copy-done.5 = bf16[128,256]{1,0:T(8,128)(2,1)S(1)} copy-done((bf16[128,256]{1,0:T(8,128)(2,1)S(1)}, bf16[128,256]{1,0:T(8,128)(2,1)}, u32[]{:S(2)}) %copy-start.5) | copy-done | bytes 65560
  7.5 66.3 %shard_map.120 = (bf16[1,256,256]{2,1,0:T(8,128)(2,1)S(1)}, f32[128,256]{1,0:T(8,128)S(1)}, f32[256,256]{1,0:T(8,128)S(1)}, f32[256,256]{1,0:T(8,128)S(1)}) custom-call(bf16[1,256,128]{2,1,0:T(8,128)(2,1)S(1)} %copy-done.4, s32[1,256]{1,0:T(1,128)S(1)} %copy-done.6, bf16[128,256]{1,0:T(8,128)(2,1)S(1)} %copy-done.5, bf16[256,256]{1,0:T(8,128)(2,1)S(1)} %copy-done.1, ...), custom_call_target="tpu_custom_call" | custom-call | tf_op jit(solution)/shard_map/pallas_call | solution.py:257
  73.8 0.7 copy.19
  74.4 0.7 copy.20
  75.1 0.7 copy.21
  75.8 0.7 copy.22
Async XLA Ops:
  0.6 0.7 copy-start.7
  1.3 0.7 copy-start.6
  2.0 1.1 %copy-start = (s32[1,10,128,128]{3,2,1,0:T(8,128)S(1)}, s32[1,10,128,128]{3,2,1,0:T(8,128)}, u32[]{:S(2)}) copy-start(s32[1,10,128,128]{3,2,1,0:T(8,128)} %counts.1) | copy-start | bytes 1966084
  3.1 0.9 %copy-start.1 = (bf16[256,256]{1,0:T(8,128)(2,1)S(1)}, bf16[256,256]{1,0:T(8,128)(2,1)}, u32[]{:S(2)}) copy-start(bf16[256,256]{1,0:T(8,128)(2,1)} %w_one.1) | copy-start | bytes 393220
  4.0 0.9 %copy-start.2 = (bf16[256,256]{1,0:T(8,128)(2,1)S(1)}, bf16[256,256]{1,0:T(8,128)(2,1)}, u32[]{:S(2)}) copy-start(bf16[256,256]{1,0:T(8,128)(2,1)} %w_two.1) | copy-start | bytes 393220
  4.9 0.9 %copy-start.3 = (bf16[1,256,256]{2,1,0:T(8,128)(2,1)S(1)}, bf16[1,256,256]{2,1,0:T(8,128)(2,1)}, u32[]{:S(2)}) copy-start(bf16[1,256,256]{2,1,0:T(8,128)(2,1)} %out_grad.1) | copy-start | bytes 393220
  5.8 0.8 %copy-start.4 = (bf16[1,256,128]{2,1,0:T(8,128)(2,1)S(1)}, bf16[1,256,128]{2,1,0:T(8,128)(2,1)}, u32[]{:S(2)}) copy-start(bf16[1,256,128]{2,1,0:T(8,128)(2,1)} %events.1) | copy-start | bytes 196612
  6.6 0.8 %copy-start.5 = (bf16[128,256]{1,0:T(8,128)(2,1)S(1)}, bf16[128,256]{1,0:T(8,128)(2,1)}, u32[]{:S(2)}) copy-start(bf16[128,256]{1,0:T(8,128)(2,1)} %w_enc.1) | copy-start | bytes 196612

commit v2 on v1

--- a/solution.py
+++ b/solution.py
@@ -38,12 +38,13 @@
 
 def step_kernel(
     scale_loss,
-    events, perm, w_enc, w_one, w_two, slots, live, counts, out_grad,
+    events_in, perm_in, w_enc_in, w_one_in, w_two_in, slots, live, counts_in, out_grad_in,
     embed, grad_enc, grad_one, grad_two,
-    adj_f, adj, adj_t, inv_deg, mid, ev_win, z_one, z_two, gs_ref, gz_ref, gh_ref,
+    events, perm, w_enc, w_one, w_two, counts, out_grad,
+    adj_f, adj, adj_t, inv_deg, mid, ev_win, z_two, gz_ref, gh_ref,
     a_src, a_dst, b_src, b_dst, qa_src, qa_dst, qb_src, qb_dst,
     rs_src, rs_dst, y_dst, x_dst, ag_dst,
-    send_sem, recv_sem,
+    load_sem, send_sem, recv_sem,
 ):
     me = lax.axis_index("dom")
     rep = lax.axis_index("rep")
@@ -62,6 +63,18 @@
     def in_x(j):
         return (rep + j) % NX
 
+    loads = [
+        pltpu.make_async_copy(src, dst, load_sem.at[i])
+        for i, (src, dst) in enumerate(
+            (
+                (perm_in, perm), (events_in, events), (counts_in, counts), (out_grad_in, out_grad),
+                (w_two_in, w_two), (w_enc_in, w_enc), (w_one_in, w_one),
+            )
+        )
+    ]
+    for load in loads:
+        load.start()
+
     barrier = pltpu.get_barrier_semaphore()
 
     def hello(device):
@@ -84,6 +97,7 @@
 
     rows = lax.broadcasted_iota(jnp.int32, (256, 256), 0)
     cols = lax.broadcasted_iota(jnp.int32, (256, 256), 1)
+    loads[0].wait()
     ids = perm[...]
     ids_row = ids.astype(F32)
     ids_col = jnp.sum(jnp.where(rows == cols, ids_row, 0.0), axis=1, keepdims=True)
@@ -91,6 +105,7 @@
     sorting = jnp.where(rows.astype(F32) == place, 1.0, 0.0).astype(BF16)
     local_col = (ids_col.astype(jnp.int32) & 255).astype(F32)
     local_rep = jnp.broadcast_to(local_col, (256, 128)).astype(BF16)
+    loads[1].wait()
     a_src[:, :, 0:128] = dot(sorting, events[0]).astype(BF16).reshape(NY, 32, 128)
     a_src[:, :, 128:256] = dot(sorting, local_rep).astype(BF16).reshape(NY, 32, 128)
 
@@ -101,6 +116,7 @@
         send(a_src.at[to], a_dst.at[my_y], 0, {"dom": to * NZ + my_z})
     a_dst[my_y] = a_src[my_y]
 
+    loads[2].wait()
     weights = []
     for s in range(10):
         row = slots[0, s, 0] - 2 * me
@@ -136,6 +152,7 @@
     inv_deg[:, 0:128] = inverse
     inv_deg[:, 128:256] = inverse
 
+    loads[3].wait()
     gs_two = (out_grad[0].astype(F32) * scale_loss * inv_deg[...]).astype(BF16)
     qa_src[0] = dot(adj_t[0:128], gs_two).astype(BF16)
     qa_src[1] = dot(adj_t[384:512], gs_two).astype(BF16)
@@ -155,6 +172,7 @@
 
     wait_for(qa_dst.at[1], recv_sem.at[1])
     wait_for(qa_dst.at[0], recv_sem.at[2])
+    loads[4].wait()
     gz_two = (gz_ref[...] + qa_dst[...].astype(F32).reshape(256, 256)).astype(BF16)
     gh_ref[...] = dot_nt(gz_two, w_two[...]) * inv_deg[...]
 
@@ -168,6 +186,9 @@
     ev_win[128:384] = dot_tn(placing, got[:, 0:128]).astype(BF16)
     send(ev_win.at[pl.ds(128, 128)], ev_win.at[pl.ds(384, 128)], 4, {"dom": left})
     send(ev_win.at[pl.ds(256, 128)], ev_win.at[pl.ds(0, 128)], 5, {"dom": right})
+
+    loads[5].wait()
+    loads[6].wait()
 
     def encoded(rows_in):
         pre_rows = dot(rows_in, w_enc[...])
@@ -253,7 +274,12 @@
 def body(events, perm, w_enc, w_one, w_two, slot_blocks, live_count, block_counts, out_grad):
     scale_loss = 1.0 / math.sqrt(lax.axis_size("rep") * lax.axis_size("dom") * events.shape[1])
     vmem = pl.BlockSpec(memory_space=pltpu.VMEM)
+    hbm = pl.BlockSpec(memory_space=pltpu.HBM)
     smem = pl.BlockSpec(memory_space=pltpu.SMEM)
+    args = [
+        pltpu.with_memory_space_constraint(x, pltpu.HBM)
+        for x in (events, perm, w_enc, w_one, w_two, block_counts, out_grad)
+    ]
     return pl.pallas_call(
         functools.partial(step_kernel, scale_loss),
         out_shape=(
@@ -262,9 +288,16 @@
             jax.ShapeDtypeStruct((256, 256), F32),
             jax.ShapeDtypeStruct((256, 256), F32),
         ),
-        in_specs=[vmem, vmem, vmem, vmem, vmem, smem, smem, vmem, vmem],
+        in_specs=[hbm, hbm, hbm, hbm, hbm, smem, smem, hbm, hbm],
         out_specs=(vmem, vmem, vmem, vmem),
         scratch_shapes=[
+            pltpu.VMEM((1, 256, 128), BF16),
+            pltpu.VMEM((1, 256), jnp.int32),
+            pltpu.VMEM((128, 256), BF16),
+            pltpu.VMEM((256, 256), BF16),
+            pltpu.VMEM((256, 256), BF16),
+            pltpu.VMEM((1, 10, 128, 128), jnp.int32),
+            pltpu.VMEM((1, 256, 256), BF16),
             pltpu.VMEM((256, 512), F32),
             pltpu.VMEM((256, 512), BF16),
             pltpu.VMEM((512, 256), BF16),
@@ -272,8 +305,6 @@
             pltpu.VMEM((256, 256), BF16),
             pltpu.VMEM((512, 128), BF16),
             pltpu.VMEM((512, 256), BF16),
-            pltpu.VMEM((512, 256), BF16),
-            pltpu.VMEM((256, 256), BF16),
             pltpu.VMEM((256, 256), F32),
             pltpu.VMEM((256, 256), F32),
             pltpu.VMEM((NY, 32, 256), BF16),
@@ -289,13 +320,14 @@
             pltpu.VMEM((NY, 16, 640), BF16),
             pltpu.VMEM((NX, 16, 640), BF16),
             pltpu.VMEM((NZ, 16, 640), BF16),
+            pltpu.SemaphoreType.DMA((7,)),
             pltpu.SemaphoreType.DMA((14,)),
             pltpu.SemaphoreType.DMA((14,)),
         ],
         compiler_params=pltpu.CompilerParams(
-            collective_id=0, has_side_effects=True, vmem_limit_bytes=32 * 1024 * 1024
+            collective_id=0, has_side_effects=True, vmem_limit_bytes=16 * 1024 * 1024
         ),
-    )(events, perm, w_enc, w_one, w_two, slot_blocks, live_count, block_counts, out_grad)
+    )(*args[:5], slot_blocks, live_count, *args[5:])
 
 
 def solution(mesh):

time: 76.8 us -> 70.6 us (0.919)
  local copies, waits for them, and re-layouts: 8.88 us -> 2.82 us
    unnamed x21 -> x7, local copies, waits for them, and re-layouts: 8.88 us -> 2.82 us
where the time goes in v2:
time: 70.6 us; the launch traced here: 70.4 us
  Pallas kernels  66.3 us (94%)
  local copies, waits for them, and re-layouts  2.82 us (4%)
  between operations  1.31 us (2%)
    pallas_call x1, Pallas kernels, body(): pl.pallas_call(functools.partial(step_kernel, scale_loss), out_shape=(jax...  66.3 us
    unnamed x7, local copies, waits for them, and re-layouts  2.82 us

profile of v2, /device:TPU:1, one launch (start us, length us, event | category | flops | bytes accessed | tf_op | source)
XLA Modules:
  0.0 70.4 jit_solution(888168594839767488)
XLA Ops:
  0.6 0.0 copy-start
  1.3 0.0 copy-done
  1.3 0.1 copy.13.slots
  1.4 66.3 %shard_map.120 = (bf16[1,256,256]{2,1,0:T(8,128)(2,1)S(1)}, f32[128,256]{1,0:T(8,128)S(1)}, f32[256,256]{1,0:T(8,128)S(1)}, f32[256,256]{1,0:T(8,128)S(1)}) custom-call(bf16[1,256,128]{2,1,0:T(8,128)(2,1)} %events_in.1, s32[1,256]{1,0:T(1,128)} %perm_in.1, bf16[128,256]{1,0:T(8,128)(2,1)} %w_enc_in.1, bf16[256,256]{1,0:T(8,128)(2,1)} %w_one_in.1, ...), custom_call_target="tpu_custom_call" | custom-call | tf_op jit(solution)/shard_map/pallas_call | solution.py:283
  67.7 0.7 copy.19
  68.4 0.7 copy.20
  69.0 0.7 copy.21
  69.7 0.7 copy.22
Async XLA Ops:
  0.6 0.7 copy-start

commit v3 on v2

--- a/solution.py
+++ b/solution.py
@@ -34,6 +34,10 @@
 
 def wait_for(ref, sem):
     pltpu.make_async_copy(ref, ref, sem).wait()
+
+
+def tile(k):
+    return 16 * (k // 2), 128 * (k % 2)
 
 
 def step_kernel(
@@ -43,7 +47,7 @@
     events, perm, w_enc, w_one, w_two, counts, out_grad,
     adj_f, adj, adj_t, inv_deg, mid, ev_win, z_two, gz_ref, gh_ref,
     a_src, a_dst, b_src, b_dst, qa_src, qa_dst, qb_src, qb_dst,
-    rs_src, rs_dst, y_dst, x_dst, ag_dst,
+    two_src, two_dst, lo_src, lo_dst, lo_mid, lo_all, hi_src, hi_dst, hi_mid, hi_all, x_dst,
     load_sem, send_sem, recv_sem,
 ):
     me = lax.axis_index("dom")
@@ -62,6 +66,22 @@
 
     def in_x(j):
         return (rep + j) % NX
+
+    core = me % 2
+    my_yc = my_y * 2 + core
+    my_zc = my_z // 2
+
+    def at_yc(k):
+        return {"dom": (k // 2) * NZ + my_zc * 2 + k % 2}
+
+    def at_zc(k):
+        return {"dom": my_y * NZ + k}
+
+    def at_y(k):
+        return {"dom": k * NZ + my_z}
+
+    def at_z(k):
+        return {"dom": my_y * NZ + k * 2 + core}
 
     loads = [
         pltpu.make_async_copy(src, dst, load_sem.at[i])
@@ -82,6 +102,7 @@
 
     for j in range(1, NY):
         hello({"dom": in_y(j) * NZ + my_z})
+        hello({"dom": in_y(j) * NZ + my_zc * 2 + 1 - core})
     for j in range(1, NZ):
         hello({"dom": my_y * NZ + in_z(j)})
     for j in range(1, NX):
@@ -109,7 +130,7 @@
     a_src[:, :, 0:128] = dot(sorting, events[0]).astype(BF16).reshape(NY, 32, 128)
     a_src[:, :, 128:256] = dot(sorting, local_rep).astype(BF16).reshape(NY, 32, 128)
 
-    pl.semaphore_wait(barrier, NY - 1 + NZ - 1 + NX - 1 + 2)
+    pl.semaphore_wait(barrier, 2 * (NY - 1) + NZ - 1 + NX - 1 + 2)
 
     for j in range(1, NY):
         to = in_y(j)
@@ -215,47 +236,73 @@
     send(qb_src.at[0], qb_dst.at[1], 8, {"dom": left})
     send(qb_src.at[1], qb_dst.at[0], 9, {"dom": right})
     gz_own = dot(adj_t[128:384], gs_one)
-    rs_src[:, :, 0:256] = dot_tn(h_one, gz_two).astype(BF16).reshape(NZ, 16, 256)
+    two_src[...] = dot_tn(h_one, gz_two).astype(BF16).reshape(NZ, 16, 256)
+    for j in range(1, NZ):
+        to = (my_yc + j) % NZ
+        send(two_src.at[to], two_dst.at[my_yc], 10, at_yc(to))
+    two_dst[my_yc] = two_src[my_yc]
 
     wait_for(qb_dst.at[1], recv_sem.at[8])
     wait_for(qb_dst.at[0], recv_sem.at[9])
     gz_one = (gz_own + qb_dst[...].astype(F32).reshape(256, 256)).astype(BF16)
-    rs_src[:, :, 256:512] = dot_tn(h_zero, gz_one).astype(BF16).reshape(NZ, 16, 256)
+    l_one = dot_tn(h_zero, gz_one).astype(BF16)
+    for k in range(NZ):
+        r, c = tile(k)
+        lo_src[k] = l_one[r : r + 16, c : c + 128]
+        hi_src[k, :, 0:128] = l_one[128 + r : 144 + r, c : c + 128]
+    for j in range(1, NZ):
+        to = (my_yc + j) % NZ
+        send(lo_src.at[to], lo_dst.at[my_yc], 11, at_yc(to))
+    lo_dst[my_yc] = lo_src[my_yc]
     gh_zero = dot_nt(gz_one, w_one[...]).astype(BF16)
     sig = sigmoid(pre)
     g_enc = (gh_zero.astype(F32) * (sig * (1.0 + pre * (1.0 - sig)))).astype(BF16)
     l_enc = dot_tn(ev_own, g_enc).astype(BF16)
     for k in range(NZ):
-        r, c = 16 * (k // 2), 128 * (k % 2)
-        rs_src[k, :, 512:640] = l_enc[r : r + 16, c : c + 128]
-
+        r, c = tile(k)
+        hi_src[k, :, 128:256] = l_enc[r : r + 16, c : c + 128]
     for j in range(1, NZ):
         to = in_z(j)
-        send(rs_src.at[to], rs_dst.at[my_z], 10, {"dom": my_y * NZ + to})
-    rs_dst[my_z] = rs_src[my_z]
+        send(hi_src.at[to], hi_dst.at[my_z], 12, at_zc(to))
+    hi_dst[my_z] = hi_src[my_z]
 
     wait_for(z_two.at[pl.ds(384, 128)], recv_sem.at[6])
     wait_for(z_two.at[pl.ds(0, 128)], recv_sem.at[7])
     embed[0] = (dot(adj[...], z_two[...]) * inv_deg[...]).astype(BF16)
 
-    wait_for(rs_dst.at[pl.ds(0, NZ - 1)], recv_sem.at[10])
-    y_dst[my_y] = jnp.sum(rs_dst[...].astype(F32), axis=0).astype(BF16)
+    wait_for(two_dst.at[pl.ds(0, NZ - 1)], recv_sem.at[10])
+    wait_for(lo_dst.at[pl.ds(0, NZ - 1)], recv_sem.at[11])
+    lo_mid[my_zc, :, 0:256] = jnp.sum(two_dst[...].astype(F32), axis=0).astype(BF16)
+    lo_mid[my_zc, :, 256:384] = jnp.sum(lo_dst[...].astype(F32), axis=0).astype(BF16)
     for j in range(1, NY):
-        send(y_dst.at[my_y], y_dst.at[my_y], 11, {"dom": in_y(j) * NZ + my_z})
-    wait_for(y_dst.at[pl.ds(0, NY - 1)], recv_sem.at[11])
-    x_dst[rep] = jnp.sum(y_dst[...].astype(F32), axis=0).astype(BF16)
+        send(lo_mid.at[my_zc], lo_mid.at[my_zc], 13, at_z((my_zc + j) % NY))
+    wait_for(hi_dst.at[pl.ds(0, NZ - 1)], recv_sem.at[12])
+    hi_mid[my_y] = jnp.sum(hi_dst[...].astype(F32), axis=0).astype(BF16)
+    for j in range(1, NY):
+        send(hi_mid.at[my_y], hi_mid.at[my_y], 14, at_y((my_y + j) % NY))
+    wait_for(lo_mid.at[pl.ds(0, NY - 1)], recv_sem.at[13])
+    x_dst[rep, :, 0:384] = jnp.sum(lo_mid[...].astype(F32), axis=0).astype(BF16)
+    wait_for(hi_mid.at[pl.ds(0, NY - 1)], recv_sem.at[14])
+    x_dst[rep, :, 384:640] = jnp.sum(hi_mid[...].astype(F32), axis=0).astype(BF16)
     for j in range(1, NX):
-        send(x_dst.at[rep], x_dst.at[rep], 12, {"rep": in_x(j)})
-    wait_for(x_dst.at[pl.ds(0, NX - 1)], recv_sem.at[12])
-    ag_dst[my_z] = jnp.sum(x_dst[...].astype(F32), axis=0).astype(BF16)
-    for j in range(1, NZ):
-        send(ag_dst.at[my_z], ag_dst.at[my_z], 13, {"dom": my_y * NZ + in_z(j)})
-    wait_for(ag_dst.at[pl.ds(0, NZ - 1)], recv_sem.at[13])
-    grad_two[...] = ag_dst[:, :, 0:256].astype(F32).reshape(256, 256)
-    grad_one[...] = ag_dst[:, :, 256:512].astype(F32).reshape(256, 256)
+        send(x_dst.at[rep], x_dst.at[rep], 15, {"rep": in_x(j)})
+    wait_for(x_dst.at[pl.ds(0, NX - 1)], recv_sem.at[15])
+    summed = jnp.sum(x_dst[...].astype(F32), axis=0).astype(BF16)
+    lo_all[my_yc] = summed[:, 0:384]
+    hi_all[my_z] = summed[:, 384:640]
+    for j in range(1, NZ):
+        send(lo_all.at[my_yc], lo_all.at[my_yc], 16, at_yc((my_yc + j) % NZ))
+        send(hi_all.at[my_z], hi_all.at[my_z], 17, at_zc(in_z(j)))
+    wait_for(hi_all.at[pl.ds(0, NZ - 1)], recv_sem.at[17])
     for k in range(NZ):
-        r, c = 16 * (k // 2), 128 * (k % 2)
-        grad_enc[r : r + 16, c : c + 128] = ag_dst[k, :, 512:640].astype(F32)
+        r, c = tile(k)
+        grad_one[128 + r : 144 + r, c : c + 128] = hi_all[k, :, 0:128].astype(F32)
+        grad_enc[r : r + 16, c : c + 128] = hi_all[k, :, 128:256].astype(F32)
+    wait_for(lo_all.at[pl.ds(0, NZ - 1)], recv_sem.at[16])
+    grad_two[...] = lo_all[:, :, 0:256].astype(F32).reshape(256, 256)
+    for k in range(NZ):
+        r, c = tile(k)
+        grad_one[r : r + 16, c : c + 128] = lo_all[k, :, 256:384].astype(F32)
 
     wait_for(a_src.at[pl.ds(0, NY - 1)], send_sem.at[0])
     wait_for(qa_src.at[0], send_sem.at[1])
@@ -265,10 +312,14 @@
         wait_for(ref.at[pl.ds(0, 128)], send_sem.at[step])
     wait_for(qb_src.at[0], send_sem.at[8])
     wait_for(qb_src.at[1], send_sem.at[9])
-    wait_for(rs_src.at[pl.ds(0, NZ - 1)], send_sem.at[10])
-    wait_for(y_dst.at[pl.ds(0, NY - 1)], send_sem.at[11])
-    wait_for(x_dst.at[pl.ds(0, NX - 1)], send_sem.at[12])
-    wait_for(ag_dst.at[pl.ds(0, NZ - 1)], send_sem.at[13])
+    wait_for(two_src.at[pl.ds(0, NZ - 1)], send_sem.at[10])
+    wait_for(lo_src.at[pl.ds(0, NZ - 1)], send_sem.at[11])
+    wait_for(hi_src.at[pl.ds(0, NZ - 1)], send_sem.at[12])
+    wait_for(lo_mid.at[pl.ds(0, NY - 1)], send_sem.at[13])
+    wait_for(hi_mid.at[pl.ds(0, NY - 1)], send_sem.at[14])
+    wait_for(x_dst.at[pl.ds(0, NX - 1)], send_sem.at[15])
+    wait_for(lo_all.at[pl.ds(0, NZ - 1)], send_sem.at[16])
+    wait_for(hi_all.at[pl.ds(0, NZ - 1)], send_sem.at[17])
 
 
 def body(events, perm, w_enc, w_one, w_two, slot_blocks, live_count, block_counts, out_grad):
@@ -315,14 +366,20 @@
             pltpu.VMEM((2, 128, 256), BF16),
             pltpu.VMEM((2, 128, 256), BF16),
             pltpu.VMEM((2, 128, 256), BF16),
-            pltpu.VMEM((NZ, 16, 640), BF16),
-            pltpu.VMEM((NZ, 16, 640), BF16),
-            pltpu.VMEM((NY, 16, 640), BF16),
+            pltpu.VMEM((NZ, 16, 256), BF16),
+            pltpu.VMEM((NZ, 16, 256), BF16),
+            pltpu.VMEM((NZ, 16, 128), BF16),
+            pltpu.VMEM((NZ, 16, 128), BF16),
+            pltpu.VMEM((NY, 16, 384), BF16),
+            pltpu.VMEM((NZ, 16, 384), BF16),
+            pltpu.VMEM((NZ, 16, 256), BF16),
+            pltpu.VMEM((NZ, 16, 256), BF16),
+            pltpu.VMEM((NY, 16, 256), BF16),
+            pltpu.VMEM((NZ, 16, 256), BF16),
             pltpu.VMEM((NX, 16, 640), BF16),
-            pltpu.VMEM((NZ, 16, 640), BF16),
             pltpu.SemaphoreType.DMA((7,)),
-            pltpu.SemaphoreType.DMA((14,)),
-            pltpu.SemaphoreType.DMA((14,)),
+            pltpu.SemaphoreType.DMA((18,)),
+            pltpu.SemaphoreType.DMA((18,)),
         ],
         compiler_params=pltpu.CompilerParams(
             collective_id=0, has_side_effects=True, vmem_limit_bytes=16 * 1024 * 1024

time: 70.6 us -> 65 us (0.921)
  Pallas kernels: 66.3 us -> 60.7 us
    pallas_call x1, Pallas kernels: 66.3 us -> 60.7 us  [body(): pl.pallas_call(functools.partial(step_kernel, scale_loss), out_shape=(jax...]
where the time goes in v3:
time: 65 us; the launch traced here: 64.9 us
  Pallas kernels  60.7 us (93%)
  local copies, waits for them, and re-layouts  2.82 us (4%)
  between operations  1.31 us (2%)
    pallas_call x1, Pallas kernels, body(): pl.pallas_call(functools.partial(step_kernel, scale_loss), out_shape=(jax...  60.7 us
    unnamed x7, local copies, waits for them, and re-layouts  2.82 us

profile of v3, /device:TPU:1, one launch (start us, length us, event | category | flops | bytes accessed | tf_op | source)
XLA Modules:
  0.0 64.9 jit_solution(16393385658216016157)
XLA Ops:
  0.6 0.0 copy-start
  1.3 0.0 copy-done
  1.3 0.1 copy.13.slots
  1.4 60.7 %shard_map.120 = (bf16[1,256,256]{2,1,0:T(8,128)(2,1)S(1)}, f32[128,256]{1,0:T(8,128)S(1)}, f32[256,256]{1,0:T(8,128)S(1)}, f32[256,256]{1,0:T(8,128)S(1)}) custom-call(bf16[1,256,128]{2,1,0:T(8,128)(2,1)} %events_in.1, s32[1,256]{1,0:T(1,128)} %perm_in.1, bf16[128,256]{1,0:T(8,128)(2,1)} %w_enc_in.1, bf16[256,256]{1,0:T(8,128)(2,1)} %w_one_in.1, ...), custom_call_target="tpu_custom_call" | custom-call | tf_op jit(solution)/shard_map/pallas_call | solution.py:334
  62.2 0.7 %copy.19 = bf16[1,256,256]{2,1,0:T(8,128)(2,1)} copy(bf16[1,256,256]{2,1,0:T(8,128)(2,1)S(1)} %get-tuple-element.8) | data formatting | bytes 262144
  62.8 0.7 %copy.20 = f32[128,256]{1,0:T(8,128)} copy(f32[128,256]{1,0:T(8,128)S(1)} %get-tuple-element.9) | data formatting | bytes 262144
  63.5 0.7 %copy.21 = f32[256,256]{1,0:T(8,128)} copy(f32[256,256]{1,0:T(8,128)S(1)} %get-tuple-element.10) | data formatting | bytes 524288
  64.2 0.7 %copy.22 = f32[256,256]{1,0:T(8,128)} copy(f32[256,256]{1,0:T(8,128)S(1)} %get-tuple-element.11) | data formatting | bytes 524288
Async XLA Ops:
  0.6 0.7 %copy-start = (s32[1,10,2]{1,2,0:T(2,128)S(1)}, s32[1,10,2]{1,2,0:T(2,128)}, u32[]{:S(2)}) copy-start(s32[1,10,2]{1,2,0:T(2,128)} %param.14) | copy-start | bytes 244

commit v4 on v2

v4 whole, which is shorter than its diff:
```python
import functools
import math

import jax
import jax.numpy as jnp
from jax import lax
from jax.experimental import pallas as pl
from jax.experimental.pallas import tpu as pltpu
from jax.sharding import PartitionSpec as P

loop_weight = 4.0
NY = 8
NZ = 16
NX = 4
F32 = jnp.float32
BF16 = jnp.bfloat16


def dot(a, b):
    return jnp.dot(a, b, preferred_element_type=F32)


def dot_nt(a, b):
    return lax.dot_general(a, b, (((1,), (1,)), ((), ())), preferred_element_type=F32)


def sigmoid(value):
    return 1.0 / (1.0 + jnp.exp(-value))


def wait_for(ref, sem):
    pltpu.make_async_copy(ref, ref, sem).wait()


def tile(k):
    return 16 * (k // 2), 128 * (k % 2)


def iota(shape, dim):
    return lax.broadcasted_iota(jnp.int32, shape, dim)


def one_where(mask):
    return jnp.where(mask, 1.0, 0.0).astype(BF16)


def step_kernel(
    scale_loss,
    events_in, perm_in, w_enc_in, w_one_in, w_two_in, slots_in, live, counts_in, out_grad_in,
    embed, grad_enc, grad_one, grad_two,
    events, perm, w_enc, w_one, w_two, counts, out_grad, slots,
    adj_f, adj, adj_t, inv_deg, mid, regroup, spread, finish, w_one_t, w_two_t,
    ev_win, z_two, gz_ref, gh_ref,
    a_src, a_dst, ai_src, ai_dst, b_src, b_dst, bi_src, bi_dst, qa_src, qa_dst, qb_src, qb_dst,
    two_src, two_dst, two_mid, two_x, two_all,
    lo_src, lo_dst, lo_mid, lo_all, hi_src, hi_dst, hi_mid, hi_all, late_x,
    load_sem, send_sem, recv_sem,
):
    me = lax.axis_index("dom")
    rep = lax.axis_index("rep")
    ndom = NY * NZ
    my_y = me // NZ
    my_z = me % NZ
    core = me % 2
    my_yc = my_y * 2 + core
    my_zc = my_z // 2
    left = {"dom": (me + ndom - 1) % ndom}
    right = {"dom": (me + 1) % ndom}

    loads = [
        pltpu.make_async_copy(src, dst, load_sem.at[i])
        for i, (src, dst) in enumerate(
            (
                (perm_in, perm), (events_in, events), (slots_in, slots), (counts_in, counts),
                (out_grad_in, out_grad), (w_two_in, w_two), (w_enc_in, w_enc), (w_one_in, w_one),
            )
        )
    ]
    for load in loads:
        load.start()

    def others(group):
        if group == "yc":
            ranks = [(my_yc + j) % NZ for j in range(1, NZ)]
            return [(k, {"dom": (k // 2) * NZ + my_zc * 2 + k % 2}) for k in ranks]
        if group == "zc":
            return [(k, {"dom": my_y * NZ + k}) for k in ((my_z + j) % NZ for j in range(1, NZ))]
        if group == "y":
            return [(k, {"dom": k * NZ + my_z}) for k in ((my_y + j) % NY for j in range(1, NY))]
        if group == "z":
            ranks = [(my_zc + j) % NY for j in range(1, NY)]
            return [(k, {"dom": my_y * NZ + k * 2 + core}) for k in ranks]
        return [(k, {"rep": k}) for k in ((rep + j) % NX for j in range(1, NX))]

    barrier = pltpu.get_barrier_semaphore()
    friends = [dev for group in ("yc", "zc", "x") for _, dev in others(group)] + [left, right]
    for device in friends:
        pl.semaphore_signal(barrier, inc=1, device_id=device, device_id_type=pl.DeviceIdType.MESH)

    def send(src, dst, step, device):
        pltpu.make_async_remote_copy(
            src_ref=src, dst_ref=dst, send_sem=send_sem.at[step], recv_sem=recv_sem.at[step],
            device_id=device, device_id_type=pl.DeviceIdType.MESH,
        ).start()

    def scatter(src, dst, mine, step, group):
        for k, device in others(group):
            send(src.at[k], dst.at[mine], step, device)
        dst[mine] = src[mine]

    def spread_out(ref, mine, step, group):
        for _, device in others(group):
            send(ref.at[mine], ref.at[mine], step, device)

    def arrived(ref, step, count):
        wait_for(ref.at[pl.ds(0, count)], recv_sem.at[step])

    def left_all(ref, step, count):
        wait_for(ref.at[pl.ds(0, count)], send_sem.at[step])

    rows = iota((256, 256), 0)
    cols = iota((256, 256), 1)
    half_rows = rows[0:128]
    half_cols = cols[0:128]
    loads[0].wait()
    ids = perm[...]
    ids_row = ids.astype(F32)
    ids_col = jnp.sum(jnp.where(rows == cols, ids_row, 0.0), axis=1, keepdims=True)
    place = jnp.sum(jnp.where(ids_col < ids_row, 1.0, 0.0), axis=0, keepdims=True).astype(jnp.int32)
    local_row = (ids & 255).astype(F32)
    id_left = jnp.where((place >> 5) == rows[0:16], local_row, 0.0).astype(BF16)
    id_right = one_where((place & 31) == half_rows)
    ai_src[...] = dot_nt(id_left, id_right)[0:NY].reshape(NY, 1, 128)
    loads[1].wait()
    a_src[...] = dot(one_where(rows == place), events[0]).astype(BF16).reshape(NY, 32, 128)

    pl.semaphore_wait(barrier, len(friends))
    scatter(ai_src, ai_dst, my_y, 1, "y")
    scatter(a_src, a_dst, my_y, 0, "y")

    loads[2].wait()
    loads[3].wait()
    weights = []
    for s in range(10):
        row = slots[0, 0, s] - 2 * me
        col = (slots[0, 1, s] - 2 * me + 1 + 2 * ndom) % (2 * ndom)
        used = s < live[0, 0]
        weights.append(
            [
                [jnp.where(used & (row == r) & (col == c), 1.0, 0.0) for c in (1, 2, 0, 3)]
                for r in range(2)
            ]
        )
    for part in range(4):
        here = slice(part * 32, part * 32 + 32)
        sums = [[None] * 4 for _ in range(2)]
        for s in range(10):
            cell = counts[0, s, here, :].astype(F32)
            for r in range(2):
                for c in range(4):
                    term = cell * weights[s][r][c]
                    sums[r][c] = term if s == 0 else sums[r][c] + term
        diag = iota((32, 128), 0) + part * 32 == iota((32, 128), 1)
        for r in range(2):
            sums[r][r] = sums[r][r] + jnp.where(diag, loop_weight, 0.0)
            for c in range(4):
                adj_f[r * 128 + part * 32 : r * 128 + part * 32 + 32, c * 128 : c * 128 + 128] = sums[r][c]
    adj[...] = adj_f[...].astype(BF16)
    for r in range(2):
        for c in range(4):
            adj_t[c * 128 : c * 128 + 128, r * 128 : r * 128 + 128] = (
                adj_f[r * 128 : r * 128 + 128, c * 128 : c * 128 + 128].T.astype(BF16)
            )
    inverse = 1.0 / dot(adj[...], jnp.ones((512, 128), BF16))
    inv_deg[:, 0:128] = inverse
    inv_deg[:, 128:256] = inverse

    loads[4].wait()
    gs_two = (out_grad[0].astype(F32) * scale_loss * inv_deg[...]).astype(BF16)
    qa_src[...] = dot(adj_t[256:512], gs_two).astype(BF16).reshape(2, 128, 256)
    send(qa_src.at[0], qa_dst.at[1], 4, left)
    send(qa_src.at[1], qa_dst.at[0], 5, right)
    gz_ref[...] = dot(adj_t[0:256], gs_two)

    source = ((rows >> 1) & (NY - 1)) * 32 + (rows >> 4) * 2 + (rows & 1)
    mid[...] = one_where(cols == source)
    regroup[...] = one_where(half_rows == (half_cols >> 4) * 2 + (half_cols & 1))
    spread[...] = one_where(half_rows == (half_cols & 15))
    loads[5].wait()
    loads[6].wait()
    loads[7].wait()
    w_two_t[...] = w_two[...].T
    w_one_t[...] = w_one[...].T

    arrived(ai_dst, 1, NY - 1)
    ids_mid = dot(ai_dst[...].reshape(NY, 128).astype(BF16), regroup[...])
    ids_mid = jnp.sum(
        jnp.where(rows[0:NY] == ((cols[0:NY] >> 1) & (NY - 1)), ids_mid, 0.0), axis=0, keepdims=True
    )
    id_left = jnp.where((cols[0:NZ] >> 4) == rows[0:NZ], ids_mid, 0.0).astype(BF16)
    bi_src[...] = dot_nt(id_left, spread[...]).reshape(NZ, 1, 128)
    scatter(bi_src, bi_dst, my_z, 3, "zc")
    arrived(a_dst, 0, NY - 1)
    b_src[...] = dot(mid[...], a_dst[...].reshape(256, 128)).astype(BF16).reshape(NZ, 16, 128)
    scatter(b_src, b_dst, my_z, 2, "zc")

    wait_for(qa_dst.at[1], recv_sem.at[4])
    wait_for(qa_dst.at[0], recv_sem.at[5])
    gz_two = (gz_ref[...] + qa_dst[...].astype(F32).reshape(256, 256)).astype(BF16)
    gh_ref[...] = dot(gz_two, w_two_t[...]) * inv_deg[...]

    arrived(bi_dst, 3, NZ - 1)
    ids_got = dot(bi_dst[...].reshape(NZ, 128).astype(BF16), spread[...])
    ids_got = jnp.sum(
        jnp.where(rows[0:NZ] == (cols[0:NZ] >> 4), ids_got, 0.0), axis=0, keepdims=True
    )
    finish[...] = one_where(rows.astype(F32) == ids_got)
    arrived(b_dst, 2, NZ - 1)
    ev_own = dot(finish[...], b_dst[...].reshape(256, 128)).astype(BF16)
    ev_win[0:256] = ev_own
    send(ev_win.at[pl.ds(0, 128)], ev_win.at[pl.ds(384, 128)], 6, left)
    send(ev_win.at[pl.ds(128, 128)], ev_win.at[pl.ds(256, 128)], 7, right)

    def encoded(rows_in):
        pre_rows = dot(rows_in, w_enc[...])
        return pre_rows, (pre_rows * sigmoid(pre_rows)).astype(BF16)

    pre, h_zero = encoded(ev_own)
    z_own = dot(h_zero, w_one[...]).astype(BF16)
    total = dot(adj[:, 0:256], z_own)
    sig = sigmoid(pre)
    enc_slope = sig * (1.0 + pre * (1.0 - sig))
    h_zero_t = h_zero.T
    ev_t = ev_own.T
    wait_for(ev_win.at[pl.ds(384, 128)], recv_sem.at[6])
    wait_for(ev_win.at[pl.ds(256, 128)], recv_sem.at[7])
    z_side = dot(encoded(ev_win[256:512])[1], w_one[...]).astype(BF16)
    agg_one = (total + dot(adj[:, 256:512], z_side)) * inv_deg[...]
    sig = sigmoid(agg_one)
    gs_one = (gh_ref[...] * (sig * (1.0 + agg_one * (1.0 - sig)))).astype(BF16)
    qb_src[...] = dot(adj_t[256:512], gs_one).astype(BF16).reshape(2, 128, 256)
    send(qb_src.at[0], qb_dst.at[1], 10, left)
    send(qb_src.at[1], qb_dst.at[0], 11, right)
    h_one = (agg_one * sig).astype(BF16)
    two_src[...] = dot(h_one.T, gz_two).astype(BF16).reshape(NZ, 16, 256)
    scatter(two_src, two_dst, my_yc, 12, "yc")
    z_two[0:256] = dot(h_one, w_two[...]).astype(BF16)
    send(z_two.at[pl.ds(0, 128)], z_two.at[pl.ds(384, 128)], 8, left)
    send(z_two.at[pl.ds(128, 128)], z_two.at[pl.ds(256, 128)], 9, right)
    gz_own = dot(adj_t[0:256], gs_one)

    wait_for(qb_dst.at[1], recv_sem.at[10])
    wait_for(qb_dst.at[0], recv_sem.at[11])
    gz_one = (gz_own + qb_dst[...].astype(F32).reshape(256, 256)).astype(BF16)
    l_one = dot(h_zero_t, gz_one).astype(BF16)
    for k in range(NZ):
        r, c = tile(k)
        lo_src[k] = l_one[r : r + 16, c : c + 128]
        hi_src[k, :, 0:128] = l_one[128 + r : 144 + r, c : c + 128]
    scatter(lo_src, lo_dst, my_yc, 13, "yc")
    gh_zero = dot(gz_one, w_one_t[...]).astype(BF16)
    g_enc = (gh_zero.astype(F32) * enc_slope).astype(BF16)
    l_enc = dot(ev_t, g_enc).astype(BF16)
    for k in range(NZ):
        r, c = tile(k)
        hi_src[k, :, 128:256] = l_enc[r : r + 16, c : c + 128]
    scatter(hi_src, hi_dst, my_z, 14, "zc")

    wait_for(z_two.at[pl.ds(384, 128)], recv_sem.at[8])
    wait_for(z_two.at[pl.ds(256, 128)], recv_sem.at[9])
    embed[0] = (dot(adj[...], z_two[...]) * inv_deg[...]).astype(BF16)

    def summed(ref):
        return jnp.sum(ref[...].astype(F32), axis=0).astype(BF16)

    arrived(two_dst, 12, NZ - 1)
    two_mid[my_zc] = summed(two_dst)
    spread_out(two_mid, my_zc, 15, "z")
    arrived(lo_dst, 13, NZ - 1)
    lo_mid[my_zc] = summed(lo_dst)
    spread_out(lo_mid, my_zc, 16, "z")
    arrived(hi_dst, 14, NZ - 1)
    hi_mid[my_y] = summed(hi_dst)
    spread_out(hi_mid, my_y, 17, "y")
    arrived(two_mid, 15, NY - 1)
    two_x[rep] = summed(two_mid)
    spread_out(two_x, rep, 18, "x")
    arrived(lo_mid, 16, NY - 1)
    late_x[rep, :, 0:128] = summed(lo_mid)
    arrived(hi_mid, 17, NY - 1)
    late_x[rep, :, 128:384] = summed(hi_mid)
    spread_out(late_x, rep, 19, "x")
    arrived(two_x, 18, NX - 1)
    two_all[my_yc] = summed(two_x)
    spread_out(two_all, my_yc, 20, "yc")
    arrived(late_x, 19, NX - 1)
    late = summed(late_x)
    hi_all[my_z] = late[:, 128:384]
    spread_out(hi_all, my_z, 22, "zc")
    lo_all[my_yc] = late[:, 0:128]
    spread_out(lo_all, my_yc, 21, "yc")
    arrived(two_all, 20, NZ - 1)
    grad_two[...] = two_all[...].astype(F32).reshape(256, 256)
    arrived(lo_all, 21, NZ - 1)
    for k in range(NZ):
        r, c = tile(k)
        grad_one[r : r + 16, c : c + 128] = lo_all[k].astype(F32)
    arrived(hi_all, 22, NZ - 1)
    for k in range(NZ):
        r, c = tile(k)
        grad_one[128 + r : 144 + r, c : c + 128] = hi_all[k, :, 0:128].astype(F32)
        grad_enc[r : r + 16, c : c + 128] = hi_all[k, :, 128:256].astype(F32)

    left_all(a_src, 0, NY - 1)
    left_all(ai_src, 1, NY - 1)
    left_all(b_src, 2, NZ - 1)
    left_all(bi_src, 3, NZ - 1)
    for step, ref in ((4, qa_src), (5, qa_src), (10, qb_src), (11, qb_src)):
        left_all(ref, step, 1)
    for step, ref in ((6, ev_win), (7, ev_win), (8, z_two), (9, z_two)):
        left_all(ref, step, 128)
    for step, ref in ((12, two_src), (13, lo_src), (14, hi_src), (20, two_all), (21, lo_all), (22, hi_all)):
        left_all(ref, step, NZ - 1)
    for step, ref in ((15, two_mid), (16, lo_mid), (17, hi_mid)):
        left_all(ref, step, NY - 1)
    left_all(two_x, 18, NX - 1)
    left_all(late_x, 19, NX - 1)


def body(events, perm, w_enc, w_one, w_two, slot_blocks, live_count, block_counts, out_grad):
    scale_loss = 1.0 / math.sqrt(lax.axis_size("rep") * lax.axis_size("dom") * events.shape[1])
    vmem = pl.BlockSpec(memory_space=pltpu.VMEM)
    smem = pl.BlockSpec(memory_space=pltpu.SMEM)
    hbm = pl.BlockSpec(memory_space=pltpu.HBM)
    slot_rows = jnp.swapaxes(slot_blocks, 1, 2)
    args = [
        pltpu.with_memory_space_constraint(x, pltpu.HBM)
        for x in (events, perm, w_enc, w_one, w_two, slot_rows, block_counts, out_grad)
    ]

    def pieces(*shape, dtype=BF16):
        return pltpu.VMEM(shape, dtype)

    return pl.pallas_call(
        functools.partial(step_kernel, scale_loss),
        out_shape=(
            jax.ShapeDtypeStruct((1, 256, 256), BF16),
            jax.ShapeDtypeStruct((128, 256), F32),
            jax.ShapeDtypeStruct((256, 256), F32),
            jax.ShapeDtypeStruct((256, 256), F32),
        ),
        in_specs=[hbm, hbm, hbm, hbm, hbm, hbm, smem, hbm, hbm],
        out_specs=(vmem, vmem, vmem, vmem),
        scratch_shapes=[
            pieces(1, 256, 128),
            pieces(1, 256, dtype=jnp.int32),
            pieces(128, 256),
            pieces(256, 256),
            pieces(256, 256),
            pieces(1, 10, 128, 128, dtype=jnp.int32),
            pieces(1, 256, 256),
            pltpu.SMEM((1, 2, 10), jnp.int32),
            pieces(256, 512, dtype=F32),
            pieces(256, 512),
            pieces(512, 256),
            pieces(256, 256, dtype=F32),
            pieces(256, 256),
            pieces(128, 256),
            pieces(128, 256),
            pieces(256, 256),
            pieces(256, 256),
            pieces(256, 256),
            pieces(512, 128),
            pieces(512, 256),
            pieces(256, 256, dtype=F32),
            pieces(256, 256, dtype=F32),
            pieces(NY, 32, 128),
            pieces(NY, 32, 128),
            pieces(NY, 1, 128, dtype=F32),
            pieces(NY, 1, 128, dtype=F32),
            pieces(NZ, 16, 128),
            pieces(NZ, 16, 128),
            pieces(NZ, 1, 128, dtype=F32),
            pieces(NZ, 1, 128, dtype=F32),
            pieces(2, 128, 256),
            pieces(2, 128, 256),
            pieces(2, 128, 256),
            pieces(2, 128, 256),
            pieces(NZ, 16, 256),
            pieces(NZ, 16, 256),
            pieces(NY, 16, 256),
            pieces(NX, 16, 256),
            pieces(NZ, 16, 256),
            pieces(NZ, 16, 128),
            pieces(NZ, 16, 128),
            pieces(NY, 16, 128),
            pieces(NZ, 16, 128),
            pieces(NZ, 16, 256),
            pieces(NZ, 16, 256),
            pieces(NY, 16, 256),
            pieces(NZ, 16, 256),
            pieces(NX, 16, 384),
            pltpu.SemaphoreType.DMA((8,)),
            pltpu.SemaphoreType.DMA((23,)),
            pltpu.SemaphoreType.DMA((23,)),
        ],
        compiler_params=pltpu.CompilerParams(
            collective_id=0, has_side_effects=True, vmem_limit_bytes=16 * 1024 * 1024
        ),
    )(*args[:6], live_count, *args[6:])


def solution(mesh):
    return jax.shard_map(
        body,
        mesh=mesh,
        in_specs=(
            P("rep", "dom", None),
            P("rep", "dom"),
            P(),
            P(),
            P(),
            P("rep", "dom", None),
            P("rep", "dom"),
            P("rep", "dom", None, None),
            P("rep", "dom", None),
        ),
        out_specs=(P("rep", "dom", None), P(), P(), P()),
        check_vma=False,
    )
```

time: 70.6 us -> 61.9 us (0.88)
  Pallas kernels: 66.3 us -> 57.7 us
    pallas_call x1, Pallas kernels: 66.3 us -> 57.7 us  [body(): pl.pallas_call(functools.partial(step_kernel, scale_loss), out_shape=(jax...]
    unnamed x7 -> x4, local copies, waits for them, and re-layouts: 2.82 us -> 2.72 us
where the time goes in v4:
time: 61.9 us; the launch traced here: 61.8 us
  Pallas kernels  57.7 us (93%)
  local copies, waits for them, and re-layouts  2.72 us (4%)
  between operations  1.29 us (2%)
    pallas_call x1, Pallas kernels, body(): pl.pallas_call(functools.partial(step_kernel, scale_loss), out_shape=(jax...  57.7 us
    unnamed x4, local copies, waits for them, and re-layouts  2.72 us

profile of v4, /device:TPU:1, one launch (start us, length us, event | category | flops | bytes accessed | tf_op | source)
XLA Modules:
  0.0 61.8 jit_solution(9463995023020631233)
XLA Ops:
  1.3 57.7 %shard_map.120 = (bf16[1,256,256]{2,1,0:T(8,128)(2,1)S(1)}, f32[128,256]{1,0:T(8,128)S(1)}, f32[256,256]{1,0:T(8,128)S(1)}, f32[256,256]{1,0:T(8,128)S(1)}) custom-call(bf16[1,256,128]{2,1,0:T(8,128)(2,1)} %events_in.1, s32[1,256]{1,0:T(1,128)} %perm_in.1, bf16[128,256]{1,0:T(8,128)(2,1)} %w_enc_in.1, bf16[256,256]{1,0:T(8,128)(2,1)} %w_one_in.1, ...), custom_call_target="tpu_custom_call" | custom-call | tf_op jit(solution)/shard_map/pallas_call | solution.py:344
  59.0 0.7 %copy.18 = bf16[1,256,256]{2,1,0:T(8,128)(2,1)} copy(bf16[1,256,256]{2,1,0:T(8,128)(2,1)S(1)} %get-tuple-element.8) | data formatting | bytes 262144
  59.7 0.7 %copy.19 = f32[128,256]{1,0:T(8,128)} copy(f32[128,256]{1,0:T(8,128)S(1)} %get-tuple-element.9) | data formatting | bytes 262144
  60.3 0.7 %copy.20 = f32[256,256]{1,0:T(8,128)} copy(f32[256,256]{1,0:T(8,128)S(1)} %get-tuple-element.10) | data formatting | bytes 524288
  61.0 0.7 %copy.21 = f32[256,256]{1,0:T(8,128)} copy(f32[256,256]{1,0:T(8,128)S(1)} %get-tuple-element.11) | data formatting | bytes 524288

commit v5 on v4

--- a/solution.py
+++ b/solution.py
@@ -30,10 +30,6 @@
 
 def wait_for(ref, sem):
     pltpu.make_async_copy(ref, ref, sem).wait()
-
-
-def tile(k):
-    return 16 * (k // 2), 128 * (k % 2)
 
 
 def iota(shape, dim):
@@ -51,9 +47,9 @@
     events, perm, w_enc, w_one, w_two, counts, out_grad, slots,
     adj_f, adj, adj_t, inv_deg, mid, regroup, spread, finish, w_one_t, w_two_t,
     ev_win, z_two, gz_ref, gh_ref,
-    a_src, a_dst, ai_src, ai_dst, b_src, b_dst, bi_src, bi_dst, qa_src, qa_dst, qb_src, qb_dst,
-    two_src, two_dst, two_mid, two_x, two_all,
-    lo_src, lo_dst, lo_mid, lo_all, hi_src, hi_dst, hi_mid, hi_all, late_x,
+    a_src, a_dst, ai_src, ai_dst, b_src, b_dst, bi_src, bi_dst, qa_src, qa_dst,
+    two_src, two_dst, two_mid, two_x, two_all, one_src, one_dst, one_mid, one_x, one_all,
+    enc_src, enc_dst, enc_y, enc_z, enc_all, h_win_t, ev_win_t, slope,
     load_sem, send_sem, recv_sem,
 ):
     me = lax.axis_index("dom")
@@ -63,6 +59,7 @@
     my_z = me % NZ
     core = me % 2
     my_yc = my_y * 2 + core
+    my_xc = rep * 2 + core
     my_zc = my_z // 2
     left = {"dom": (me + ndom - 1) % ndom}
     right = {"dom": (me + 1) % ndom}
@@ -90,10 +87,13 @@
         if group == "z":
             ranks = [(my_zc + j) % NY for j in range(1, NY)]
             return [(k, {"dom": my_y * NZ + k * 2 + core}) for k in ranks]
+        if group == "xc":
+            ranks = [(my_xc + j) % NY for j in range(1, NY)]
+            return [(k, {"dom": me - core + k % 2, "rep": k // 2}) for k in ranks]
         return [(k, {"rep": k}) for k in ((rep + j) % NX for j in range(1, NX))]
 
     barrier = pltpu.get_barrier_semaphore()
-    friends = [dev for group in ("yc", "zc", "x") for _, dev in others(group)] + [left, right]
+    friends = [dev for group in ("yc", "zc", "xc") for _, dev in others(group)] + [left, right]
     for device in friends:
         pl.semaphore_signal(barrier, inc=1, device_id=device, device_id_type=pl.DeviceIdType.MESH)
 
@@ -229,102 +229,88 @@
     z_own = dot(h_zero, w_one[...]).astype(BF16)
     total = dot(adj[:, 0:256], z_own)
     sig = sigmoid(pre)
-    enc_slope = sig * (1.0 + pre * (1.0 - sig))
-    h_zero_t = h_zero.T
-    ev_t = ev_own.T
+    slope[0:256] = sig * (1.0 + pre * (1.0 - sig))
+    h_win_t[:, 0:256] = h_zero.T
+    ev_win_t[:, 0:256] = ev_own.T
     wait_for(ev_win.at[pl.ds(384, 128)], recv_sem.at[6])
     wait_for(ev_win.at[pl.ds(256, 128)], recv_sem.at[7])
-    z_side = dot(encoded(ev_win[256:512])[1], w_one[...]).astype(BF16)
+    ev_side = ev_win[256:512]
+    pre, h_zero = encoded(ev_side)
+    z_side = dot(h_zero, w_one[...]).astype(BF16)
     agg_one = (total + dot(adj[:, 256:512], z_side)) * inv_deg[...]
+    h_win_t[:, 256:512] = h_zero.T
+    ev_win_t[:, 256:512] = ev_side.T
+    sig = sigmoid(pre)
+    slope[256:512] = sig * (1.0 + pre * (1.0 - sig))
+
     sig = sigmoid(agg_one)
     gs_one = (gh_ref[...] * (sig * (1.0 + agg_one * (1.0 - sig)))).astype(BF16)
-    qb_src[...] = dot(adj_t[256:512], gs_one).astype(BF16).reshape(2, 128, 256)
-    send(qb_src.at[0], qb_dst.at[1], 10, left)
-    send(qb_src.at[1], qb_dst.at[0], 11, right)
+    gz_one = dot(adj_t[...], gs_one).astype(BF16)
+    one_src[...] = dot(h_win_t[...], gz_one).astype(BF16).reshape(NZ, 16, 256)
+    scatter(one_src, one_dst, my_z, 10, "zc")
     h_one = (agg_one * sig).astype(BF16)
     two_src[...] = dot(h_one.T, gz_two).astype(BF16).reshape(NZ, 16, 256)
-    scatter(two_src, two_dst, my_yc, 12, "yc")
+    scatter(two_src, two_dst, my_yc, 11, "yc")
+    gh_zero = dot(gz_one, w_one_t[...]).astype(BF16)
+    g_enc = (gh_zero.astype(F32) * slope[...]).astype(BF16)
+    enc_src[...] = dot(ev_win_t[...], g_enc).astype(BF16).reshape(NY, 16, 256)
+    scatter(enc_src, enc_dst, my_xc, 12, "xc")
     z_two[0:256] = dot(h_one, w_two[...]).astype(BF16)
     send(z_two.at[pl.ds(0, 128)], z_two.at[pl.ds(384, 128)], 8, left)
     send(z_two.at[pl.ds(128, 128)], z_two.at[pl.ds(256, 128)], 9, right)
-    gz_own = dot(adj_t[0:256], gs_one)
-
-    wait_for(qb_dst.at[1], recv_sem.at[10])
-    wait_for(qb_dst.at[0], recv_sem.at[11])
-    gz_one = (gz_own + qb_dst[...].astype(F32).reshape(256, 256)).astype(BF16)
-    l_one = dot(h_zero_t, gz_one).astype(BF16)
-    for k in range(NZ):
-        r, c = tile(k)
-        lo_src[k] = l_one[r : r + 16, c : c + 128]
-        hi_src[k, :, 0:128] = l_one[128 + r : 144 + r, c : c + 128]
-    scatter(lo_src, lo_dst, my_yc, 13, "yc")
-    gh_zero = dot(gz_one, w_one_t[...]).astype(BF16)
-    g_enc = (gh_zero.astype(F32) * enc_slope).astype(BF16)
-    l_enc = dot(ev_t, g_enc).astype(BF16)
-    for k in range(NZ):
-        r, c = tile(k)
-        hi_src[k, :, 128:256] = l_enc[r : r + 16, c : c + 128]
-    scatter(hi_src, hi_dst, my_z, 14, "zc")
-
+
+    def summed(ref):
+        return jnp.sum(ref[...].astype(F32), axis=0).astype(BF16)
+
+    arrived(enc_dst, 12, NY - 1)
+    enc_y[my_y] = summed(enc_dst)
+    spread_out(enc_y, my_y, 13, "y")
+    arrived(one_dst, 10, NZ - 1)
+    one_mid[my_y] = summed(one_dst)
+    spread_out(one_mid, my_y, 14, "y")
+    arrived(two_dst, 11, NZ - 1)
+    two_mid[my_zc] = summed(two_dst)
+    spread_out(two_mid, my_zc, 15, "z")
     wait_for(z_two.at[pl.ds(384, 128)], recv_sem.at[8])
     wait_for(z_two.at[pl.ds(256, 128)], recv_sem.at[9])
     embed[0] = (dot(adj[...], z_two[...]) * inv_deg[...]).astype(BF16)
-
-    def summed(ref):
-        return jnp.sum(ref[...].astype(F32), axis=0).astype(BF16)
-
-    arrived(two_dst, 12, NZ - 1)
-    two_mid[my_zc] = summed(two_dst)
-    spread_out(two_mid, my_zc, 15, "z")
-    arrived(lo_dst, 13, NZ - 1)
-    lo_mid[my_zc] = summed(lo_dst)
-    spread_out(lo_mid, my_zc, 16, "z")
-    arrived(hi_dst, 14, NZ - 1)
-    hi_mid[my_y] = summed(hi_dst)
-    spread_out(hi_mid, my_y, 17, "y")
+    arrived(enc_y, 13, NY - 1)
+    enc_z[my_zc] = summed(enc_y)
+    spread_out(enc_z, my_zc, 16, "z")
+    arrived(one_mid, 14, NY - 1)
+    one_x[rep] = summed(one_mid)
+    spread_out(one_x, rep, 17, "x")
     arrived(two_mid, 15, NY - 1)
     two_x[rep] = summed(two_mid)
     spread_out(two_x, rep, 18, "x")
-    arrived(lo_mid, 16, NY - 1)
-    late_x[rep, :, 0:128] = summed(lo_mid)
-    arrived(hi_mid, 17, NY - 1)
-    late_x[rep, :, 128:384] = summed(hi_mid)
-    spread_out(late_x, rep, 19, "x")
+    arrived(one_x, 17, NX - 1)
+    one_all[my_z] = summed(one_x)
+    spread_out(one_all, my_z, 19, "zc")
     arrived(two_x, 18, NX - 1)
     two_all[my_yc] = summed(two_x)
     spread_out(two_all, my_yc, 20, "yc")
-    arrived(late_x, 19, NX - 1)
-    late = summed(late_x)
-    hi_all[my_z] = late[:, 128:384]
-    spread_out(hi_all, my_z, 22, "zc")
-    lo_all[my_yc] = late[:, 0:128]
-    spread_out(lo_all, my_yc, 21, "yc")
+    arrived(enc_z, 16, NY - 1)
+    enc_all[my_xc] = summed(enc_z)
+    spread_out(enc_all, my_xc, 21, "xc")
+    arrived(enc_all, 21, NY - 1)
+    grad_enc[...] = enc_all[...].astype(F32).reshape(128, 256)
+    arrived(one_all, 19, NZ - 1)
+    grad_one[...] = one_all[...].astype(F32).reshape(256, 256)
     arrived(two_all, 20, NZ - 1)
     grad_two[...] = two_all[...].astype(F32).reshape(256, 256)
-    arrived(lo_all, 21, NZ - 1)
-    for k in range(NZ):
-        r, c = tile(k)
-        grad_one[r : r + 16, c : c + 128] = lo_all[k].astype(F32)
-    arrived(hi_all, 22, NZ - 1)
-    for k in range(NZ):
-        r, c = tile(k)
-        grad_one[128 + r : 144 + r, c : c + 128] = hi_all[k, :, 0:128].astype(F32)
-        grad_enc[r : r + 16, c : c + 128] = hi_all[k, :, 128:256].astype(F32)
-
-    left_all(a_src, 0, NY - 1)
-    left_all(ai_src, 1, NY - 1)
-    left_all(b_src, 2, NZ - 1)
-    left_all(bi_src, 3, NZ - 1)
-    for step, ref in ((4, qa_src), (5, qa_src), (10, qb_src), (11, qb_src)):
+
+    for step, ref in ((0, a_src), (1, ai_src), (13, enc_y), (14, one_mid), (15, two_mid), (16, enc_z)):
+        left_all(ref, step, NY - 1)
+    for step, ref in ((2, b_src), (3, bi_src), (10, one_src), (11, two_src), (19, one_all), (20, two_all)):
+        left_all(ref, step, NZ - 1)
+    for step, ref in ((12, enc_src), (21, enc_all)):
+        left_all(ref, step, NY - 1)
+    for step, ref in ((17, one_x), (18, two_x)):
+        left_all(ref, step, NX - 1)
+    for step, ref in ((4, qa_src), (5, qa_src)):
         left_all(ref, step, 1)
     for step, ref in ((6, ev_win), (7, ev_win), (8, z_two), (9, z_two)):
         left_all(ref, step, 128)
-    for step, ref in ((12, two_src), (13, lo_src), (14, hi_src), (20, two_all), (21, lo_all), (22, hi_all)):
-        left_all(ref, step, NZ - 1)
-    for step, ref in ((15, two_mid), (16, lo_mid), (17, hi_mid)):
-        left_all(ref, step, NY - 1)
-    left_all(two_x, 18, NX - 1)
-    left_all(late_x, 19, NX - 1)
 
 
 def body(events, perm, w_enc, w_one, w_two, slot_blocks, live_count, block_counts, out_grad):
@@ -384,25 +370,27 @@
             pieces(NZ, 1, 128, dtype=F32),
             pieces(2, 128, 256),
             pieces(2, 128, 256),
-            pieces(2, 128, 256),
-            pieces(2, 128, 256),
             pieces(NZ, 16, 256),
             pieces(NZ, 16, 256),
             pieces(NY, 16, 256),
             pieces(NX, 16, 256),
             pieces(NZ, 16, 256),
-            pieces(NZ, 16, 128),
-            pieces(NZ, 16, 128),
-            pieces(NY, 16, 128),
-            pieces(NZ, 16, 128),
-            pieces(NZ, 16, 256),
-            pieces(NZ, 16, 256),
-            pieces(NY, 16, 256),
-            pieces(NZ, 16, 256),
-            pieces(NX, 16, 384),
+            pieces(NZ, 16, 256),
+            pieces(NZ, 16, 256),
+            pieces(NY, 16, 256),
+            pieces(NX, 16, 256),
+            pieces(NZ, 16, 256),
+            pieces(NY, 16, 256),
+            pieces(NY, 16, 256),
+            pieces(NY, 16, 256),
+            pieces(NY, 16, 256),
+            pieces(NY, 16, 256),
+            pieces(256, 512),
+            pieces(128, 512),
+            pieces(512, 256, dtype=F32),
             pltpu.SemaphoreType.DMA((8,)),
-            pltpu.SemaphoreType.DMA((23,)),
-            pltpu.SemaphoreType.DMA((23,)),
+            pltpu.SemaphoreType.DMA((22,)),
+            pltpu.SemaphoreType.DMA((22,)),
         ],
         compiler_params=pltpu.CompilerParams(
             collective_id=0, has_side_effects=True, vmem_limit_bytes=16 * 1024 * 1024

time: 61.9 us -> 56.7 us (0.916)
  Pallas kernels: 57.7 us -> 52.5 us
    pallas_call x1, Pallas kernels: 57.7 us -> 52.5 us  [body(): pl.pallas_call(functools.partial(step_kernel, scale_loss), out_shape=(jax...]
where the time goes in v5:
time: 56.7 us; the launch traced here: 56.5 us
  Pallas kernels  52.5 us (93%)
  local copies, waits for them, and re-layouts  2.72 us (5%)
  between operations  1.29 us (2%)
    pallas_call x1, Pallas kernels, body(): pl.pallas_call(functools.partial(step_kernel, scale_loss), out_shape=(jax...  52.5 us
    unnamed x4, local copies, waits for them, and re-layouts  2.72 us

profile of v5, /device:TPU:1, one launch (start us, length us, event | category | flops | bytes accessed | tf_op | source)
XLA Modules:
  0.0 56.5 jit_solution(10814115631872902127)
XLA Ops:
  1.3 52.5 %shard_map.120 = (bf16[1,256,256]{2,1,0:T(8,128)(2,1)S(1)}, f32[128,256]{1,0:T(8,128)S(1)}, f32[256,256]{1,0:T(8,128)S(1)}, f32[256,256]{1,0:T(8,128)S(1)}) custom-call(bf16[1,256,128]{2,1,0:T(8,128)(2,1)} %events_in.1, s32[1,256]{1,0:T(1,128)} %perm_in.1, bf16[128,256]{1,0:T(8,128)(2,1)} %w_enc_in.1, bf16[256,256]{1,0:T(8,128)(2,1)} %w_one_in.1, ...), custom_call_target="tpu_custom_call" | custom-call | tf_op jit(solution)/shard_map/pallas_call | solution.py:330
  53.8 0.7 %copy.18 = bf16[1,256,256]{2,1,0:T(8,128)(2,1)} copy(bf16[1,256,256]{2,1,0:T(8,128)(2,1)S(1)} %get-tuple-element.8) | data formatting | bytes 262144
  54.5 0.7 %copy.19 = f32[128,256]{1,0:T(8,128)} copy(f32[128,256]{1,0:T(8,128)S(1)} %get-tuple-element.9) | data formatting | bytes 262144
  55.1 0.7 %copy.20 = f32[256,256]{1,0:T(8,128)} copy(f32[256,256]{1,0:T(8,128)S(1)} %get-tuple-element.10) | data formatting | bytes 524288
  55.8 0.7 %copy.21 = f32[256,256]{1,0:T(8,128)} copy(f32[256,256]{1,0:T(8,128)S(1)} %get-tuple-element.11) | data formatting | bytes 524288

commit v6 on v5

--- a/solution.py
+++ b/solution.py
@@ -43,13 +43,13 @@
 def step_kernel(
     scale_loss,
     events_in, perm_in, w_enc_in, w_one_in, w_two_in, slots_in, live, counts_in, out_grad_in,
-    embed, grad_enc, grad_one, grad_two,
+    embed, enc_all, one_all, two_all,
     events, perm, w_enc, w_one, w_two, counts, out_grad, slots,
     adj_f, adj, adj_t, inv_deg, mid, regroup, spread, finish, w_one_t, w_two_t,
     ev_win, z_two, gz_ref, gh_ref,
     a_src, a_dst, ai_src, ai_dst, b_src, b_dst, bi_src, bi_dst, qa_src, qa_dst,
-    two_src, two_dst, two_mid, two_x, two_all, one_src, one_dst, one_mid, one_x, one_all,
-    enc_src, enc_dst, enc_y, enc_z, enc_all, h_win_t, ev_win_t, slope,
+    two_src, two_dst, two_mid, two_x, one_src, one_dst, one_mid, one_x,
+    enc_src, enc_dst, enc_y, enc_z, h_win_t, ev_win_t, slope,
     load_sem, send_sem, recv_sem,
 ):
     me = lax.axis_index("dom")
@@ -77,20 +77,20 @@
         load.start()
 
     def others(group):
-        if group == "yc":
-            ranks = [(my_yc + j) % NZ for j in range(1, NZ)]
-            return [(k, {"dom": (k // 2) * NZ + my_zc * 2 + k % 2}) for k in ranks]
-        if group == "zc":
-            return [(k, {"dom": my_y * NZ + k}) for k in ((my_z + j) % NZ for j in range(1, NZ))]
-        if group == "y":
-            return [(k, {"dom": k * NZ + my_z}) for k in ((my_y + j) % NY for j in range(1, NY))]
-        if group == "z":
-            ranks = [(my_zc + j) % NY for j in range(1, NY)]
-            return [(k, {"dom": my_y * NZ + k * 2 + core}) for k in ranks]
-        if group == "xc":
-            ranks = [(my_xc + j) % NY for j in range(1, NY)]
-            return [(k, {"dom": me - core + k % 2, "rep": k // 2}) for k in ranks]
-        return [(k, {"rep": k}) for k in ((rep + j) % NX for j in range(1, NX))]
+        ring = NX if group[0] == "x" else NY
+        here = {"x": rep, "y": my_y, "z": my_zc}[group[0]]
+        found = []
+        for ahead in sorted(range(ring), key=lambda n: -min(n, ring - n)):
+            chip = (here + ahead) % ring
+            for flip in range(len(group)):
+                if ahead or flip:
+                    side = (core + flip) % 2
+                    y = chip if group[0] == "y" else my_y
+                    z = chip if group[0] == "z" else my_zc
+                    x = chip if group[0] == "x" else rep
+                    rank = chip * 2 + side if len(group) == 2 else chip
+                    found.append((rank, {"dom": y * NZ + z * 2 + side, "rep": x}))
+        return found
 
     barrier = pltpu.get_barrier_semaphore()
     friends = [dev for group in ("yc", "zc", "xc") for _, dev in others(group)] + [left, right]
@@ -293,11 +293,8 @@
     enc_all[my_xc] = summed(enc_z)
     spread_out(enc_all, my_xc, 21, "xc")
     arrived(enc_all, 21, NY - 1)
-    grad_enc[...] = enc_all[...].astype(F32).reshape(128, 256)
     arrived(one_all, 19, NZ - 1)
-    grad_one[...] = one_all[...].astype(F32).reshape(256, 256)
     arrived(two_all, 20, NZ - 1)
-    grad_two[...] = two_all[...].astype(F32).reshape(256, 256)
 
     for step, ref in ((0, a_src), (1, ai_src), (13, enc_y), (14, one_mid), (15, two_mid), (16, enc_z)):
         left_all(ref, step, NY - 1)
@@ -313,6 +310,21 @@
         left_all(ref, step, 128)
 
 
+def result_kernel(
+    embed, enc_all, one_all, two_all, embed_out, grad_enc, grad_one, grad_two, enc, one, two, sem
+):
+    stores = [pltpu.make_async_copy(embed, embed_out, sem.at[0])]
+    stores[0].start()
+    for i, (src, wide, out) in enumerate(
+        ((enc_all, enc, grad_enc), (one_all, one, grad_one), (two_all, two, grad_two))
+    ):
+        wide[...] = src[...].astype(F32).reshape(wide.shape)
+        stores.append(pltpu.make_async_copy(wide, out, sem.at[i + 1]))
+        stores[-1].start()
+    for store in stores:
+        store.wait()
+
+
 def body(events, perm, w_enc, w_one, w_two, slot_blocks, live_count, block_counts, out_grad):
     scale_loss = 1.0 / math.sqrt(lax.axis_size("rep") * lax.axis_size("dom") * events.shape[1])
     vmem = pl.BlockSpec(memory_space=pltpu.VMEM)
@@ -327,15 +339,15 @@
     def pieces(*shape, dtype=BF16):
         return pltpu.VMEM(shape, dtype)
 
-    return pl.pallas_call(
+    found = pl.pallas_call(
         functools.partial(step_kernel, scale_loss),
         out_shape=(
             jax.ShapeDtypeStruct((1, 256, 256), BF16),
-            jax.ShapeDtypeStruct((128, 256), F32),
-            jax.ShapeDtypeStruct((256, 256), F32),
-            jax.ShapeDtypeStruct((256, 256), F32),
+            jax.ShapeDtypeStruct((NY, 16, 256), BF16),
+            jax.ShapeDtypeStruct((NZ, 16, 256), BF16),
+            jax.ShapeDtypeStruct((NZ, 16, 256), BF16),
         ),
-        in_specs=[hbm, hbm, hbm, hbm, hbm, hbm, smem, hbm, hbm],
+        in_specs=[hbm] * 6 + [smem] + [hbm] * 2,
         out_specs=(vmem, vmem, vmem, vmem),
         scratch_shapes=[
             pieces(1, 256, 128),
@@ -376,11 +388,8 @@
             pieces(NX, 16, 256),
             pieces(NZ, 16, 256),
             pieces(NZ, 16, 256),
-            pieces(NZ, 16, 256),
             pieces(NY, 16, 256),
             pieces(NX, 16, 256),
-            pieces(NZ, 16, 256),
-            pieces(NY, 16, 256),
             pieces(NY, 16, 256),
             pieces(NY, 16, 256),
             pieces(NY, 16, 256),
@@ -396,6 +405,24 @@
             collective_id=0, has_side_effects=True, vmem_limit_bytes=16 * 1024 * 1024
         ),
     )(*args[:6], live_count, *args[6:])
+    return pl.pallas_call(
+        result_kernel,
+        out_shape=(
+            jax.ShapeDtypeStruct((1, 256, 256), BF16),
+            jax.ShapeDtypeStruct((128, 256), F32),
+            jax.ShapeDtypeStruct((256, 256), F32),
+            jax.ShapeDtypeStruct((256, 256), F32),
+        ),
+        in_specs=[vmem] * 4,
+        out_specs=(pl.BlockSpec(memory_space=pl.ANY),) * 4,
+        scratch_shapes=[
+            pieces(128, 256, dtype=F32),
+            pieces(256, 256, dtype=F32),
+            pieces(256, 256, dtype=F32),
+            pltpu.SemaphoreType.DMA((4,)),
+        ],
+        compiler_params=pltpu.CompilerParams(vmem_limit_bytes=8 * 1024 * 1024),
+    )(*found)
 
 
 def solution(mesh):

time: 56.7 us -> 51.4 us (0.907)
  local copies, waits for them, and re-layouts: 2.72 us -> 0 us
  Pallas kernels: 52.5 us -> 49.9 us
    pallas_call x1, Pallas kernels: 52.5 us -> 49 us  [body(): pl.pallas_call(functools.partial(step_kernel, scale_loss), out_shape=(jax...]
    unnamed x4 -> x0, local copies, waits for them, and re-layouts: 2.72 us -> none
    pallas_call x0 -> x1, Pallas kernels: none -> 0.91 us  [body(): pl.pallas_call(result_kernel, out_shape=(jax.ShapeDtypeStruct((1, 256, 25...]
where the time goes in v6:
time: 51.4 us; the launch traced here: 51.2 us
  Pallas kernels  49.9 us (97%)
  between operations  1.29 us (3%)
    pallas_call x1, Pallas kernels, body(): pl.pallas_call(functools.partial(step_kernel, scale_loss), out_shape=(jax...  49 us

profile of v6, /device:TPU:1, one launch (start us, length us, event | category | flops | bytes accessed | tf_op | source)
XLA Modules:
  0.0 51.2 jit_solution(11841216190452966368)
XLA Ops:
  1.3 49.0 %shard_map.120 = (bf16[1,256,256]{2,1,0:T(8,128)(2,1)S(1)}, bf16[8,16,256]{2,1,0:T(8,128)(2,1)S(1)}, bf16[16,16,256]{2,1,0:T(8,128)(2,1)S(1)}, bf16[16,16,256]{2,1,0:T(8,128)(2,1)S(1)}) custom-call(bf16[1,256,128]{2,1,0:T(8,128)(2,1)} %events_in.1, s32[1,256]{1,0:T(1,128)} %perm_in.1, bf16[128,256]{1,0:T(8,128)(2,1)} %w_enc_in.1, bf16[256,256]{1,0:T(8,128)(2,1)} %w_one_in.1, ...), custom_call_target="tpu_custom_call" | custom-call | tf_op jit(solution)/shard_map/pallas_call | solution.py:342
  50.3 0.9 %shard_map.121 = (bf16[1,256,256]{2,1,0:T(8,128)(2,1)}, f32[128,256]{1,0:T(8,128)}, f32[256,256]{1,0:T(8,128)}, f32[256,256]{1,0:T(8,128)}) custom-call(bf16[1,256,256]{2,1,0:T(8,128)(2,1)S(1)} %get-tuple-element.8.embed, bf16[8,16,256]{2,1,0:T(8,128)(2,1)S(1)} %get-tuple-element.9.enc_all, bf16[16,16,256]{2,1,0:T(8,128)(2,1)S(1)} %get-tuple-element.10.one_all, ...), custom_call_target="tpu_custom_call" | custom-call | tf_op jit(solution)/shard_map/pallas_call | solution.py:408

commit v7 on v6

--- a/solution.py
+++ b/solution.py
@@ -73,7 +73,7 @@
             )
         )
     ]
-    for load in loads:
+    for load in loads[:2]:
         load.start()
 
     def others(group):
@@ -89,13 +89,24 @@
                     z = chip if group[0] == "z" else my_zc
                     x = chip if group[0] == "x" else rep
                     rank = chip * 2 + side if len(group) == 2 else chip
-                    found.append((rank, {"dom": y * NZ + z * 2 + side, "rep": x}))
+                    found.append((min(ahead, ring - ahead), rank, {"dom": y * NZ + z * 2 + side, "rep": x}))
         return found
 
     barrier = pltpu.get_barrier_semaphore()
-    friends = [dev for group in ("yc", "zc", "xc") for _, dev in others(group)] + [left, right]
-    for device in friends:
+
+    def hello(device):
         pl.semaphore_signal(barrier, inc=1, device_id=device, device_id_type=pl.DeviceIdType.MESH)
+
+    friends = others("y") + others("zc") + [f for f in others("xc") if f[0]]
+    friends.sort(key=lambda f: -f[0])
+    for _, _, device in friends:
+        hello(device)
+    at_start = my_z == 0
+    at_end = my_z == NZ - 1
+    pl.when(at_start)(lambda: hello(left))
+    pl.when(at_end)(lambda: hello(right))
+    for load in loads[2:]:
+        load.start()
 
     def send(src, dst, step, device):
         pltpu.make_async_remote_copy(
@@ -104,12 +115,12 @@
         ).start()
 
     def scatter(src, dst, mine, step, group):
-        for k, device in others(group):
+        for _, k, device in others(group):
             send(src.at[k], dst.at[mine], step, device)
         dst[mine] = src[mine]
 
     def spread_out(ref, mine, step, group):
-        for _, device in others(group):
+        for _, _, device in others(group):
             send(ref.at[mine], ref.at[mine], step, device)
 
     def arrived(ref, step, count):
@@ -134,7 +145,8 @@
     loads[1].wait()
     a_src[...] = dot(one_where(rows == place), events[0]).astype(BF16).reshape(NY, 32, 128)
 
-    pl.semaphore_wait(barrier, len(friends))
+    edge = jnp.where(at_start | at_end, 1, 0)
+    pl.semaphore_wait(barrier, len(friends) + edge)
     scatter(ai_src, ai_dst, my_y, 1, "y")
     scatter(a_src, a_dst, my_y, 0, "y")
 

time: 51.4 us -> 51.3 us (level)
  no operation moved by 1% of the time
where the time goes in v7:
time: 51.3 us; the launch traced here: 51.1 us
  Pallas kernels  49.8 us (97%)
  between operations  1.29 us (3%)
    pallas_call x1, Pallas kernels, body(): pl.pallas_call(functools.partial(step_kernel, scale_loss), out_shape=(jax...  48.9 us

profile of v7, /device:TPU:1, one launch (start us, length us, event | category | flops | bytes accessed | tf_op | source)
XLA Modules:
  0.0 51.1 jit_solution(2186641487519950759)
XLA Ops:
  1.3 48.9 %shard_map.120 = (bf16[1,256,256]{2,1,0:T(8,128)(2,1)S(1)}, bf16[8,16,256]{2,1,0:T(8,128)(2,1)S(1)}, bf16[16,16,256]{2,1,0:T(8,128)(2,1)S(1)}, bf16[16,16,256]{2,1,0:T(8,128)(2,1)S(1)}) custom-call(bf16[1,256,128]{2,1,0:T(8,128)(2,1)} %events_in.1, s32[1,256]{1,0:T(1,128)} %perm_in.1, bf16[128,256]{1,0:T(8,128)(2,1)} %w_enc_in.1, bf16[256,256]{1,0:T(8,128)(2,1)} %w_one_in.1, ...), custom_call_target="tpu_custom_call" | custom-call | tf_op jit(solution)/shard_map/pallas_call | solution.py:354
  50.2 0.9 %shard_map.121 = (bf16[1,256,256]{2,1,0:T(8,128)(2,1)}, f32[128,256]{1,0:T(8,128)}, f32[256,256]{1,0:T(8,128)}, f32[256,256]{1,0:T(8,128)}) custom-call(bf16[1,256,256]{2,1,0:T(8,128)(2,1)S(1)} %get-tuple-element.8.embed, bf16[8,16,256]{2,1,0:T(8,128)(2,1)S(1)} %get-tuple-element.9.enc_all, bf16[16,16,256]{2,1,0:T(8,128)(2,1)S(1)} %get-tuple-element.10.one_all, ...), custom_call_target="tpu_custom_call" | custom-call | tf_op jit(solution)/shard_map/pallas_call | solution.py:420

commit v8 on v7

--- a/solution.py
+++ b/solution.py
@@ -114,10 +114,14 @@
             device_id=device, device_id_type=pl.DeviceIdType.MESH,
         ).start()
 
-    def scatter(src, dst, mine, step, group):
-        for _, k, device in others(group):
-            send(src.at[k], dst.at[mine], step, device)
-        dst[mine] = src[mine]
+    def scatter(*flows):
+        starts = []
+        for src, dst, mine, step, group in flows:
+            starts += [(away, src.at[k], dst.at[mine], step, dev) for away, k, dev in others(group)]
+        for _, src, dst, step, device in sorted(starts, key=lambda start: -start[0]):
+            send(src, dst, step, device)
+        for src, dst, mine, _, _ in flows:
+            dst[mine] = src[mine]
 
     def spread_out(ref, mine, step, group):
         for _, _, device in others(group):
@@ -147,8 +151,7 @@
 
     edge = jnp.where(at_start | at_end, 1, 0)
     pl.semaphore_wait(barrier, len(friends) + edge)
-    scatter(ai_src, ai_dst, my_y, 1, "y")
-    scatter(a_src, a_dst, my_y, 0, "y")
+    scatter((ai_src, ai_dst, my_y, 1, "y"), (a_src, a_dst, my_y, 0, "y"))
 
     loads[2].wait()
     loads[3].wait()
@@ -211,10 +214,9 @@
     )
     id_left = jnp.where((cols[0:NZ] >> 4) == rows[0:NZ], ids_mid, 0.0).astype(BF16)
     bi_src[...] = dot_nt(id_left, spread[...]).reshape(NZ, 1, 128)
-    scatter(bi_src, bi_dst, my_z, 3, "zc")
     arrived(a_dst, 0, NY - 1)
     b_src[...] = dot(mid[...], a_dst[...].reshape(256, 128)).astype(BF16).reshape(NZ, 16, 128)
-    scatter(b_src, b_dst, my_z, 2, "zc")
+    scatter((bi_src, bi_dst, my_z, 3, "zc"), (b_src, b_dst, my_z, 2, "zc"))
 
     wait_for(qa_dst.at[1], recv_sem.at[4])
     wait_for(qa_dst.at[0], recv_sem.at[5])
@@ -259,17 +261,14 @@
     gs_one = (gh_ref[...] * (sig * (1.0 + agg_one * (1.0 - sig)))).astype(BF16)
     gz_one = dot(adj_t[...], gs_one).astype(BF16)
     one_src[...] = dot(h_win_t[...], gz_one).astype(BF16).reshape(NZ, 16, 256)
-    scatter(one_src, one_dst, my_z, 10, "zc")
     h_one = (agg_one * sig).astype(BF16)
     two_src[...] = dot(h_one.T, gz_two).astype(BF16).reshape(NZ, 16, 256)
-    scatter(two_src, two_dst, my_yc, 11, "yc")
+    scatter((one_src, one_dst, my_z, 10, "zc"), (two_src, two_dst, my_yc, 11, "yc"))
     gh_zero = dot(gz_one, w_one_t[...]).astype(BF16)
     g_enc = (gh_zero.astype(F32) * slope[...]).astype(BF16)
     enc_src[...] = dot(ev_win_t[...], g_enc).astype(BF16).reshape(NY, 16, 256)
-    scatter(enc_src, enc_dst, my_xc, 12, "xc")
+    scatter((enc_src, enc_dst, my_xc, 12, "xc"))
     z_two[0:256] = dot(h_one, w_two[...]).astype(BF16)
-    send(z_two.at[pl.ds(0, 128)], z_two.at[pl.ds(384, 128)], 8, left)
-    send(z_two.at[pl.ds(128, 128)], z_two.at[pl.ds(256, 128)], 9, right)
 
     def summed(ref):
         return jnp.sum(ref[...].astype(F32), axis=0).astype(BF16)
@@ -283,9 +282,8 @@
     arrived(two_dst, 11, NZ - 1)
     two_mid[my_zc] = summed(two_dst)
     spread_out(two_mid, my_zc, 15, "z")
-    wait_for(z_two.at[pl.ds(384, 128)], recv_sem.at[8])
-    wait_for(z_two.at[pl.ds(256, 128)], recv_sem.at[9])
-    embed[0] = (dot(adj[...], z_two[...]) * inv_deg[...]).astype(BF16)
+    send(z_two.at[pl.ds(0, 128)], z_two.at[pl.ds(384, 128)], 8, left)
+    send(z_two.at[pl.ds(128, 128)], z_two.at[pl.ds(256, 128)], 9, right)
     arrived(enc_y, 13, NY - 1)
     enc_z[my_zc] = summed(enc_y)
     spread_out(enc_z, my_zc, 16, "z")
@@ -295,6 +293,9 @@
     arrived(two_mid, 15, NY - 1)
     two_x[rep] = summed(two_mid)
     spread_out(two_x, rep, 18, "x")
+    wait_for(z_two.at[pl.ds(384, 128)], recv_sem.at[8])
+    wait_for(z_two.at[pl.ds(256, 128)], recv_sem.at[9])
+    embed[0] = (dot(adj[...], z_two[...]) * inv_deg[...]).astype(BF16)
     arrived(one_x, 17, NX - 1)
     one_all[my_z] = summed(one_x)
     spread_out(one_all, my_z, 19, "zc")

time: 51.3 us -> 51.5 us (level)
  no operation moved by 1% of the time
where the time goes in v8:
time: 51.5 us; the launch traced here: 51.3 us
  Pallas kernels  50 us (97%)
  between operations  1.29 us (3%)
    pallas_call x1, Pallas kernels, body(): pl.pallas_call(functools.partial(step_kernel, scale_loss), out_shape=(jax...  49.1 us

profile of v8, /device:TPU:1, one launch (start us, length us, event | category | flops | bytes accessed | tf_op | source)
XLA Modules:
  0.0 51.3 jit_solution(11909286971014209722)
XLA Ops:
  1.3 49.1 %shard_map.120 = (bf16[1,256,256]{2,1,0:T(8,128)(2,1)S(1)}, bf16[8,16,256]{2,1,0:T(8,128)(2,1)S(1)}, bf16[16,16,256]{2,1,0:T(8,128)(2,1)S(1)}, bf16[16,16,256]{2,1,0:T(8,128)(2,1)S(1)}) custom-call(bf16[1,256,128]{2,1,0:T(8,128)(2,1)} %events_in.1, s32[1,256]{1,0:T(1,128)} %perm_in.1, bf16[128,256]{1,0:T(8,128)(2,1)} %w_enc_in.1, bf16[256,256]{1,0:T(8,128)(2,1)} %w_one_in.1, ...), custom_call_target="tpu_custom_call" | custom-call | tf_op jit(solution)/shard_map/pallas_call | solution.py:355
  50.4 0.9 %shard_map.121 = (bf16[1,256,256]{2,1,0:T(8,128)(2,1)}, f32[128,256]{1,0:T(8,128)}, f32[256,256]{1,0:T(8,128)}, f32[256,256]{1,0:T(8,128)}) custom-call(bf16[1,256,256]{2,1,0:T(8,128)(2,1)S(1)} %get-tuple-element.8.embed, bf16[8,16,256]{2,1,0:T(8,128)(2,1)S(1)} %get-tuple-element.9.enc_all, bf16[16,16,256]{2,1,0:T(8,128)(2,1)S(1)} %get-tuple-element.10.one_all, ...), custom_call_target="tpu_custom_call" | custom-call | tf_op jit(solution)/shard_map/pallas_call | solution.py:421

commit v9 on v8

--- a/solution.py
+++ b/solution.py
@@ -47,7 +47,7 @@
     events, perm, w_enc, w_one, w_two, counts, out_grad, slots,
     adj_f, adj, adj_t, inv_deg, mid, regroup, spread, finish, w_one_t, w_two_t,
     ev_win, z_two, gz_ref, gh_ref,
-    a_src, a_dst, ai_src, ai_dst, b_src, b_dst, bi_src, bi_dst, qa_src, qa_dst,
+    a_src, a_dst, ai_src, ai_dst, b_src, b_dst, bi_src, bi_dst, edge, edge_i, far_rows, far_ids, qa_src, qa_dst,
     two_src, two_dst, two_mid, two_x, one_src, one_dst, one_mid, one_x,
     enc_src, enc_dst, enc_y, enc_z, h_win_t, ev_win_t, slope,
     load_sem, send_sem, recv_sem,
@@ -149,8 +149,8 @@
     loads[1].wait()
     a_src[...] = dot(one_where(rows == place), events[0]).astype(BF16).reshape(NY, 32, 128)
 
-    edge = jnp.where(at_start | at_end, 1, 0)
-    pl.semaphore_wait(barrier, len(friends) + edge)
+    extra = jnp.where(at_start | at_end, 1, 0)
+    pl.semaphore_wait(barrier, len(friends) + extra)
     scatter((ai_src, ai_dst, my_y, 1, "y"), (a_src, a_dst, my_y, 0, "y"))
 
     loads[2].wait()
@@ -213,27 +213,58 @@
         jnp.where(rows[0:NY] == ((cols[0:NY] >> 1) & (NY - 1)), ids_mid, 0.0), axis=0, keepdims=True
     )
     id_left = jnp.where((cols[0:NZ] >> 4) == rows[0:NZ], ids_mid, 0.0).astype(BF16)
-    bi_src[...] = dot_nt(id_left, spread[...]).reshape(NZ, 1, 128)
+    bi_src[1:17] = dot_nt(id_left, spread[...]).reshape(NZ, 1, 128)
     arrived(a_dst, 0, NY - 1)
-    b_src[...] = dot(mid[...], a_dst[...].reshape(256, 128)).astype(BF16).reshape(NZ, 16, 128)
-    scatter((bi_src, bi_dst, my_z, 3, "zc"), (b_src, b_dst, my_z, 2, "zc"))
+    b_src[1:17] = dot(mid[...], a_dst[...].reshape(256, 128)).astype(BF16).reshape(NZ, 16, 128)
+    for ref in (b_src, bi_src):
+        ref[0] = ref[NZ]
+        ref[NZ + 1] = ref[1]
+    up = {"dom": ((my_y + 1) % NY) * NZ}
+    down = {"dom": ((my_y + NY - 1) % NY) * NZ + NZ - 1}
+    for src, dst, step in ((bi_src, edge_i, 23), (b_src, edge, 22)):
+        send(src.at[NZ], dst.at[my_z], step, up)
+        send(src.at[1], dst.at[my_z], step, down)
+    for _, k, device in others("zc"):
+        send(bi_src.at[pl.ds(k + k % 2, 2)], bi_dst.at[my_z], 3, device)
+        send(b_src.at[pl.ds(k + k % 2, 2)], b_dst.at[my_z], 2, device)
+    bi_dst[my_z] = bi_src[pl.ds(my_z + core, 2)]
+    b_dst[my_z] = b_src[pl.ds(my_z + core, 2)]
 
     wait_for(qa_dst.at[1], recv_sem.at[4])
     wait_for(qa_dst.at[0], recv_sem.at[5])
     gz_two = (gz_ref[...] + qa_dst[...].astype(F32).reshape(256, 256)).astype(BF16)
     gh_ref[...] = dot(gz_two, w_two_t[...]) * inv_deg[...]
 
+    def lane_ids(found):
+        found = dot(found.astype(BF16), spread[...])
+        return jnp.sum(jnp.where(rows[0:NZ] == (cols[0:NZ] >> 4), found, 0.0), axis=0, keepdims=True)
+
+    low = core == 0
     arrived(bi_dst, 3, NZ - 1)
-    ids_got = dot(bi_dst[...].reshape(NZ, 128).astype(BF16), spread[...])
-    ids_got = jnp.sum(
-        jnp.where(rows[0:NZ] == (cols[0:NZ] >> 4), ids_got, 0.0), axis=0, keepdims=True
+    first = bi_dst[:, 0].reshape(NZ, 128)
+    second = bi_dst[:, 1].reshape(NZ, 128)
+    far_ids[...] = jnp.where(low, first, second)
+    finish[...] = one_where(rows.astype(F32) == lane_ids(jnp.where(low, second, first)))
+    arrived(b_dst, 2, NZ - 1)
+    first = b_dst[:, 0].reshape(256, 128)
+    second = b_dst[:, 1].reshape(256, 128)
+    far_rows[...] = jnp.where(low, first, second)
+    ev_own = dot(finish[...], jnp.where(low, second, first)).astype(BF16)
+    ev_win[0:256] = ev_own
+    send(
+        ev_win.at[pl.ds(128 * (1 - core), 128)], ev_win.at[pl.ds(256 + 128 * core, 128)], 6,
+        {"dom": me + 1 - 2 * core},
     )
-    finish[...] = one_where(rows.astype(F32) == ids_got)
-    arrived(b_dst, 2, NZ - 1)
-    ev_own = dot(finish[...], b_dst[...].reshape(256, 128)).astype(BF16)
-    ev_win[0:256] = ev_own
-    send(ev_win.at[pl.ds(0, 128)], ev_win.at[pl.ds(384, 128)], 6, left)
-    send(ev_win.at[pl.ds(128, 128)], ev_win.at[pl.ds(256, 128)], 7, right)
+
+    @pl.when(at_start | at_end)
+    def _():
+        arrived(edge_i, 23, NZ)
+        far_ids[...] = edge_i[...].reshape(NZ, 128)
+        arrived(edge, 22, NZ)
+        far_rows[...] = edge[...].reshape(256, 128)
+
+    far_place = one_where((half_rows + 128 * (1 - core)).astype(F32) == lane_ids(far_ids[...]))
+    ev_win[pl.ds(256 + 128 * core, 128)] = dot(far_place, far_rows[...]).astype(BF16)
 
     def encoded(rows_in):
         pre_rows = dot(rows_in, w_enc[...])
@@ -246,8 +277,7 @@
     slope[0:256] = sig * (1.0 + pre * (1.0 - sig))
     h_win_t[:, 0:256] = h_zero.T
     ev_win_t[:, 0:256] = ev_own.T
-    wait_for(ev_win.at[pl.ds(384, 128)], recv_sem.at[6])
-    wait_for(ev_win.at[pl.ds(256, 128)], recv_sem.at[7])
+    wait_for(ev_win.at[pl.ds(384 - 128 * core, 128)], recv_sem.at[6])
     ev_side = ev_win[256:512]
     pre, h_zero = encoded(ev_side)
     z_side = dot(h_zero, w_one[...]).astype(BF16)
@@ -311,7 +341,7 @@
 
     for step, ref in ((0, a_src), (1, ai_src), (13, enc_y), (14, one_mid), (15, two_mid), (16, enc_z)):
         left_all(ref, step, NY - 1)
-    for step, ref in ((2, b_src), (3, bi_src), (10, one_src), (11, two_src), (19, one_all), (20, two_all)):
+    for step, ref in ((2, b_dst), (3, bi_dst), (10, one_src), (11, two_src), (19, one_all), (20, two_all)):
         left_all(ref, step, NZ - 1)
     for step, ref in ((12, enc_src), (21, enc_all)):
         left_all(ref, step, NY - 1)
@@ -319,7 +349,9 @@
         left_all(ref, step, NX - 1)
     for step, ref in ((4, qa_src), (5, qa_src)):
         left_all(ref, step, 1)
-    for step, ref in ((6, ev_win), (7, ev_win), (8, z_two), (9, z_two)):
+    left_all(b_src, 22, 2)
+    left_all(bi_src, 23, 2)
+    for step, ref in ((6, ev_win), (8, z_two), (9, z_two)):
         left_all(ref, step, 128)
 
 
@@ -389,10 +421,14 @@
             pieces(NY, 32, 128),
             pieces(NY, 1, 128, dtype=F32),
             pieces(NY, 1, 128, dtype=F32),
-            pieces(NZ, 16, 128),
+            pieces(NZ + 2, 16, 128),
+            pieces(NZ, 2, 16, 128),
+            pieces(NZ + 2, 1, 128, dtype=F32),
+            pieces(NZ, 2, 1, 128, dtype=F32),
             pieces(NZ, 16, 128),
             pieces(NZ, 1, 128, dtype=F32),
-            pieces(NZ, 1, 128, dtype=F32),
+            pieces(256, 128),
+            pieces(NZ, 128, dtype=F32),
             pieces(2, 128, 256),
             pieces(2, 128, 256),
             pieces(NZ, 16, 256),
@@ -411,8 +447,8 @@
             pieces(128, 512),
             pieces(512, 256, dtype=F32),
             pltpu.SemaphoreType.DMA((8,)),
-            pltpu.SemaphoreType.DMA((22,)),
-            pltpu.SemaphoreType.DMA((22,)),
+            pltpu.SemaphoreType.DMA((24,)),
+            pltpu.SemaphoreType.DMA((24,)),
         ],
         compiler_params=pltpu.CompilerParams(
             collective_id=0, has_side_effects=True, vmem_limit_bytes=16 * 1024 * 1024

time: 51.5 us -> 50.2 us (0.975)
  Pallas kernels: 50 us -> 48.7 us
    pallas_call x1, Pallas kernels: 49.1 us -> 47.8 us  [body(): pl.pallas_call(functools.partial(step_kernel, scale_loss), out_shape=(jax...]
where the time goes in v9:
time: 50.2 us; the launch traced here: 50 us
  Pallas kernels  48.7 us (97%)
  between operations  1.29 us (3%)
    pallas_call x1, Pallas kernels, body(): pl.pallas_call(functools.partial(step_kernel, scale_loss), out_shape=(jax...  47.8 us

profile of v9, /device:TPU:1, one launch (start us, length us, event | category | flops | bytes accessed | tf_op | source)
XLA Modules:
  0.0 50.0 jit_solution(472007041797186184)
XLA Ops:
  1.3 47.8 %shard_map.120 = (bf16[1,256,256]{2,1,0:T(8,128)(2,1)S(1)}, bf16[8,16,256]{2,1,0:T(8,128)(2,1)S(1)}, bf16[16,16,256]{2,1,0:T(8,128)(2,1)S(1)}, bf16[16,16,256]{2,1,0:T(8,128)(2,1)S(1)}) custom-call(bf16[1,256,128]{2,1,0:T(8,128)(2,1)} %events_in.1, s32[1,256]{1,0:T(1,128)} %perm_in.1, bf16[128,256]{1,0:T(8,128)(2,1)} %w_enc_in.1, bf16[256,256]{1,0:T(8,128)(2,1)} %w_one_in.1, ...), custom_call_target="tpu_custom_call" | custom-call | tf_op jit(solution)/shard_map/pallas_call | solution.py:387
  49.1 0.9 %shard_map.121 = (bf16[1,256,256]{2,1,0:T(8,128)(2,1)}, f32[128,256]{1,0:T(8,128)}, f32[256,256]{1,0:T(8,128)}, f32[256,256]{1,0:T(8,128)}) custom-call(bf16[1,256,256]{2,1,0:T(8,128)(2,1)S(1)} %get-tuple-element.8.embed, bf16[8,16,256]{2,1,0:T(8,128)(2,1)S(1)} %get-tuple-element.9.enc_all, bf16[16,16,256]{2,1,0:T(8,128)(2,1)S(1)} %get-tuple-element.10.one_all, ...), custom_call_target="tpu_custom_call" | custom-call | tf_op jit(solution)/shard_map/pallas_call | solution.py:457

commit v10 on v9

--- a/solution.py
+++ b/solution.py
@@ -43,12 +43,13 @@
 def step_kernel(
     scale_loss,
     events_in, perm_in, w_enc_in, w_one_in, w_two_in, slots_in, live, counts_in, out_grad_in,
-    embed, enc_all, one_all, two_all,
+    embed, enc_all, one_a_all, one_b_all, two_a_all, two_b_all,
     events, perm, w_enc, w_one, w_two, counts, out_grad, slots,
     adj_f, adj, adj_t, inv_deg, mid, regroup, spread, finish, w_one_t, w_two_t,
     ev_win, z_two, gz_ref, gh_ref,
     a_src, a_dst, ai_src, ai_dst, b_src, b_dst, bi_src, bi_dst, edge, edge_i, far_rows, far_ids, qa_src, qa_dst,
-    two_src, two_dst, two_mid, two_x, one_src, one_dst, one_mid, one_x,
+    two_a_src, two_a_dst, two_a_mid, two_b_src, two_b_dst, two_b_mid, two_x,
+    one_a_src, one_a_dst, one_a_mid, one_b_src, one_b_dst, one_b_mid, one_x,
     enc_src, enc_dst, enc_y, enc_z, h_win_t, ev_win_t, slope,
     load_sem, send_sem, recv_sem,
 ):
@@ -123,9 +124,12 @@
         for src, dst, mine, _, _ in flows:
             dst[mine] = src[mine]
 
-    def spread_out(ref, mine, step, group):
-        for _, _, device in others(group):
-            send(ref.at[mine], ref.at[mine], step, device)
+    def spread_out(*flows):
+        starts = []
+        for ref, mine, step, group in flows:
+            starts += [(away, ref.at[mine], step, dev) for away, _, dev in others(group)]
+        for _, piece, step, device in sorted(starts, key=lambda start: -start[0]):
+            send(piece, piece, step, device)
 
     def arrived(ref, step, count):
         wait_for(ref.at[pl.ds(0, count)], recv_sem.at[step])
@@ -288,12 +292,17 @@
     slope[256:512] = sig * (1.0 + pre * (1.0 - sig))
 
     sig = sigmoid(agg_one)
+    h_one = (agg_one * sig).astype(BF16)
+    grad = dot(h_one.T, gz_two).astype(BF16).reshape(NZ, 16, 256)
+    two_a_src[...] = grad[:, :, 0:128]
+    two_b_src[...] = grad[:, :, 128:256]
+    scatter((two_a_src, two_a_dst, my_yc, 24, "yc"), (two_b_src, two_b_dst, my_z, 25, "zc"))
     gs_one = (gh_ref[...] * (sig * (1.0 + agg_one * (1.0 - sig)))).astype(BF16)
     gz_one = dot(adj_t[...], gs_one).astype(BF16)
-    one_src[...] = dot(h_win_t[...], gz_one).astype(BF16).reshape(NZ, 16, 256)
-    h_one = (agg_one * sig).astype(BF16)
-    two_src[...] = dot(h_one.T, gz_two).astype(BF16).reshape(NZ, 16, 256)
-    scatter((one_src, one_dst, my_z, 10, "zc"), (two_src, two_dst, my_yc, 11, "yc"))
+    grad = dot(h_win_t[...], gz_one).astype(BF16).reshape(NZ, 16, 256)
+    one_a_src[...] = grad[:, :, 0:128]
+    one_b_src[...] = grad[:, :, 128:256]
+    scatter((one_a_src, one_a_dst, my_yc, 10, "yc"), (one_b_src, one_b_dst, my_z, 11, "zc"))
     gh_zero = dot(gz_one, w_one_t[...]).astype(BF16)
     g_enc = (gh_zero.astype(F32) * slope[...]).astype(BF16)
     enc_src[...] = dot(ev_win_t[...], g_enc).astype(BF16).reshape(NY, 16, 256)
@@ -303,45 +312,65 @@
     def summed(ref):
         return jnp.sum(ref[...].astype(F32), axis=0).astype(BF16)
 
+    arrived(two_a_dst, 24, NZ - 1)
+    two_a_mid[my_zc] = summed(two_a_dst)
+    spread_out((two_a_mid, my_zc, 14, "z"))
+    arrived(two_b_dst, 25, NZ - 1)
+    two_b_mid[my_y] = summed(two_b_dst)
+    spread_out((two_b_mid, my_y, 15, "y"))
     arrived(enc_dst, 12, NY - 1)
     enc_y[my_y] = summed(enc_dst)
-    spread_out(enc_y, my_y, 13, "y")
-    arrived(one_dst, 10, NZ - 1)
-    one_mid[my_y] = summed(one_dst)
-    spread_out(one_mid, my_y, 14, "y")
-    arrived(two_dst, 11, NZ - 1)
-    two_mid[my_zc] = summed(two_dst)
-    spread_out(two_mid, my_zc, 15, "z")
+    spread_out((enc_y, my_y, 13, "y"))
+    arrived(one_a_dst, 10, NZ - 1)
+    one_a_mid[my_zc] = summed(one_a_dst)
+    spread_out((one_a_mid, my_zc, 26, "z"))
+    arrived(one_b_dst, 11, NZ - 1)
+    one_b_mid[my_y] = summed(one_b_dst)
+    spread_out((one_b_mid, my_y, 27, "y"))
     send(z_two.at[pl.ds(0, 128)], z_two.at[pl.ds(384, 128)], 8, left)
     send(z_two.at[pl.ds(128, 128)], z_two.at[pl.ds(256, 128)], 9, right)
+    arrived(two_a_mid, 14, NY - 1)
+    two_x[rep, :, 0:128] = summed(two_a_mid)
+    arrived(two_b_mid, 15, NY - 1)
+    two_x[rep, :, 128:256] = summed(two_b_mid)
+    spread_out((two_x, rep, 18, "x"))
     arrived(enc_y, 13, NY - 1)
     enc_z[my_zc] = summed(enc_y)
-    spread_out(enc_z, my_zc, 16, "z")
-    arrived(one_mid, 14, NY - 1)
-    one_x[rep] = summed(one_mid)
-    spread_out(one_x, rep, 17, "x")
-    arrived(two_mid, 15, NY - 1)
-    two_x[rep] = summed(two_mid)
-    spread_out(two_x, rep, 18, "x")
+    spread_out((enc_z, my_zc, 16, "z"))
+    arrived(one_a_mid, 26, NY - 1)
+    one_x[rep, :, 0:128] = summed(one_a_mid)
+    arrived(one_b_mid, 27, NY - 1)
+    one_x[rep, :, 128:256] = summed(one_b_mid)
+    spread_out((one_x, rep, 17, "x"))
+    arrived(two_x, 18, NX - 1)
+    total = summed(two_x)
+    two_a_all[my_yc] = total[:, 0:128]
+    two_b_all[my_z] = total[:, 128:256]
+    spread_out((two_a_all, my_yc, 20, "yc"), (two_b_all, my_z, 28, "zc"))
+    arrived(one_x, 17, NX - 1)
+    total = summed(one_x)
+    one_a_all[my_yc] = total[:, 0:128]
+    one_b_all[my_z] = total[:, 128:256]
+    spread_out((one_a_all, my_yc, 19, "yc"), (one_b_all, my_z, 29, "zc"))
+    arrived(enc_z, 16, NY - 1)
+    enc_all[my_xc] = summed(enc_z)
+    spread_out((enc_all, my_xc, 21, "xc"))
     wait_for(z_two.at[pl.ds(384, 128)], recv_sem.at[8])
     wait_for(z_two.at[pl.ds(256, 128)], recv_sem.at[9])
     embed[0] = (dot(adj[...], z_two[...]) * inv_deg[...]).astype(BF16)
-    arrived(one_x, 17, NX - 1)
-    one_all[my_z] = summed(one_x)
-    spread_out(one_all, my_z, 19, "zc")
-    arrived(two_x, 18, NX - 1)
-    two_all[my_yc] = summed(two_x)
-    spread_out(two_all, my_yc, 20, "yc")
-    arrived(enc_z, 16, NY - 1)
-    enc_all[my_xc] = summed(enc_z)
-    spread_out(enc_all, my_xc, 21, "xc")
+    arrived(two_a_all, 20, NZ - 1)
+    arrived(two_b_all, 28, NZ - 1)
     arrived(enc_all, 21, NY - 1)
-    arrived(one_all, 19, NZ - 1)
-    arrived(two_all, 20, NZ - 1)
-
-    for step, ref in ((0, a_src), (1, ai_src), (13, enc_y), (14, one_mid), (15, two_mid), (16, enc_z)):
+    arrived(one_a_all, 19, NZ - 1)
+    arrived(one_b_all, 29, NZ - 1)
+
+    for step, ref in ((0, a_src), (1, ai_src), (13, enc_y), (16, enc_z)):
         left_all(ref, step, NY - 1)
-    for step, ref in ((2, b_dst), (3, bi_dst), (10, one_src), (11, two_src), (19, one_all), (20, two_all)):
+    for step, ref in ((14, two_a_mid), (15, two_b_mid), (26, one_a_mid), (27, one_b_mid)):
+        left_all(ref, step, NY - 1)
+    for step, ref in ((2, b_dst), (3, bi_dst), (10, one_a_src), (11, one_b_src), (19, one_a_all), (29, one_b_all)):
+        left_all(ref, step, NZ - 1)
+    for step, ref in ((24, two_a_src), (25, two_b_src), (20, two_a_all), (28, two_b_all)):
         left_all(ref, step, NZ - 1)
     for step, ref in ((12, enc_src), (21, enc_all)):
         left_all(ref, step, NY - 1)
@@ -356,16 +385,21 @@
 
 
 def result_kernel(
-    embed, enc_all, one_all, two_all, embed_out, grad_enc, grad_one, grad_two, enc, one, two, sem
+    embed, enc_all, one_a, one_b, two_a, two_b, embed_out, grad_enc, grad_one, grad_two, enc, one, two, sem
 ):
     stores = [pltpu.make_async_copy(embed, embed_out, sem.at[0])]
     stores[0].start()
-    for i, (src, wide, out) in enumerate(
-        ((enc_all, enc, grad_enc), (one_all, one, grad_one), (two_all, two, grad_two))
-    ):
-        wide[...] = src[...].astype(F32).reshape(wide.shape)
-        stores.append(pltpu.make_async_copy(wide, out, sem.at[i + 1]))
-        stores[-1].start()
+    one[:, 0:128] = one_a[...].astype(F32).reshape(256, 128)
+    one[:, 128:256] = one_b[...].astype(F32).reshape(256, 128)
+    stores.append(pltpu.make_async_copy(one, grad_one, sem.at[1]))
+    stores[1].start()
+    two[:, 0:128] = two_a[...].astype(F32).reshape(256, 128)
+    two[:, 128:256] = two_b[...].astype(F32).reshape(256, 128)
+    stores.append(pltpu.make_async_copy(two, grad_two, sem.at[2]))
+    stores[2].start()
+    enc[...] = enc_all[...].astype(F32).reshape(128, 256)
+    stores.append(pltpu.make_async_copy(enc, grad_enc, sem.at[3]))
+    stores[3].start()
     for store in stores:
         store.wait()
 
@@ -389,11 +423,13 @@
         out_shape=(
             jax.ShapeDtypeStruct((1, 256, 256), BF16),
             jax.ShapeDtypeStruct((NY, 16, 256), BF16),
-            jax.ShapeDtypeStruct((NZ, 16, 256), BF16),
-            jax.ShapeDtypeStruct((NZ, 16, 256), BF16),
+            jax.ShapeDtypeStruct((NZ, 16, 128), BF16),
+            jax.ShapeDtypeStruct((NZ, 16, 128), BF16),
+            jax.ShapeDtypeStruct((NZ, 16, 128), BF16),
+            jax.ShapeDtypeStruct((NZ, 16, 128), BF16),
         ),
         in_specs=[hbm] * 6 + [smem] + [hbm] * 2,
-        out_specs=(vmem, vmem, vmem, vmem),
+        out_specs=(vmem,) * 6,
         scratch_shapes=[
             pieces(1, 256, 128),
             pieces(1, 256, dtype=jnp.int32),
@@ -431,13 +467,19 @@
             pieces(NZ, 128, dtype=F32),
             pieces(2, 128, 256),
             pieces(2, 128, 256),
-            pieces(NZ, 16, 256),
-            pieces(NZ, 16, 256),
-            pieces(NY, 16, 256),
+            pieces(NZ, 16, 128),
+            pieces(NZ, 16, 128),
+            pieces(NY, 16, 128),
+            pieces(NZ, 16, 128),
+            pieces(NZ, 16, 128),
+            pieces(NY, 16, 128),
             pieces(NX, 16, 256),
-            pieces(NZ, 16, 256),
-            pieces(NZ, 16, 256),
-            pieces(NY, 16, 256),
+            pieces(NZ, 16, 128),
+            pieces(NZ, 16, 128),
+            pieces(NY, 16, 128),
+            pieces(NZ, 16, 128),
+            pieces(NZ, 16, 128),
+            pieces(NY, 16, 128),
             pieces(NX, 16, 256),
             pieces(NY, 16, 256),
             pieces(NY, 16, 256),
@@ -447,8 +489,8 @@
             pieces(128, 512),
             pieces(512, 256, dtype=F32),
             pltpu.SemaphoreType.DMA((8,)),
-            pltpu.SemaphoreType.DMA((24,)),
-            pltpu.SemaphoreType.DMA((24,)),
+            pltpu.SemaphoreType.DMA((30,)),
+            pltpu.SemaphoreType.DMA((30,)),
         ],
         compiler_params=pltpu.CompilerParams(
             collective_id=0, has_side_effects=True, vmem_limit_bytes=16 * 1024 * 1024
@@ -462,7 +504,7 @@
             jax.ShapeDtypeStruct((256, 256), F32),
             jax.ShapeDtypeStruct((256, 256), F32),
         ),
-        in_specs=[vmem] * 4,
+        in_specs=[vmem] * 6,
         out_specs=(pl.BlockSpec(memory_space=pl.ANY),) * 4,
         scratch_shapes=[
             pieces(128, 256, dtype=F32),

time: 50.2 us -> 50.7 us (level)
  Pallas kernels: 48.7 us -> 49.3 us
    pallas_call x1, Pallas kernels: 47.8 us -> 48.4 us  [body(): pl.pallas_call(functools.partial(step_kernel, scale_loss), out_shape=(jax...]
where the time goes in v10:
time: 50.7 us; the launch traced here: 50.6 us
  Pallas kernels  49.3 us (97%)
  between operations  1.29 us (3%)
    pallas_call x1, Pallas kernels, body(): pl.pallas_call(functools.partial(step_kernel, scale_loss), out_shape=(jax...  48.4 us

profile of v10, /device:TPU:1, one launch (start us, length us, event | category | flops | bytes accessed | tf_op | source)
XLA Modules:
  0.0 50.6 jit_solution(15820876493521570466)
XLA Ops:
  1.3 48.4 %shard_map.120 = (bf16[1,256,256]{2,1,0:T(8,128)(2,1)S(1)}, bf16[8,16,256]{2,1,0:T(8,128)(2,1)S(1)}, bf16[16,16,128]{2,1,0:T(8,128)(2,1)S(1)}, bf16[16,16,128]{2...) custom-call(bf16[1,256,128]{2,1,0:T(8,128)(2,1)} %events_in.1, ...), custom_call_target="tpu_custom_call" | custom-call | tf_op jit(solution)/shard_map/pallas_call | solution.py:421
  49.6 0.9 %shard_map.121 = (bf16[1,256,256]{2,1,0:T(8,128)(2,1)}, f32[128,256]{1,0:T(8,128)}, f32[256,256]{1,0:T(8,128)}, f32[256,256]{1,0:T(8,128)}) custom-call(bf16[1,256,256]{2,1,0:T(8,128)(2,1)S(1)} %get-tuple-element.10.embed, bf16[8,16,256]{2,1,0:T(8,128)(2,1)S(1)} %get-tuple-element.11.enc_all, bf16[16,16,128]{2,1,0:T(8,128)(2,1)S(1)} %get-tuple-element.12.one_a, ...), custom_call_target="tpu_custom_call" | custom-call | tf_op jit(solution)/shard_map/pallas_call | solution.py:499

commit v11 on v9

--- a/solution.py
+++ b/solution.py
@@ -48,7 +48,8 @@
     adj_f, adj, adj_t, inv_deg, mid, regroup, spread, finish, w_one_t, w_two_t,
     ev_win, z_two, gz_ref, gh_ref,
     a_src, a_dst, ai_src, ai_dst, b_src, b_dst, bi_src, bi_dst, edge, edge_i, far_rows, far_ids, qa_src, qa_dst,
-    two_src, two_dst, two_mid, two_x, one_src, one_dst, one_mid, one_x,
+    two_f, two_give, two_take, two_src, two_dst, two_mid, two_x,
+    one_f, one_give, one_take, one_src, one_dst, one_mid, one_x,
     enc_src, enc_dst, enc_y, enc_z, h_win_t, ev_win_t, slope,
     load_sem, send_sem, recv_sem,
 ):
@@ -63,6 +64,7 @@
     my_zc = my_z // 2
     left = {"dom": (me + ndom - 1) % ndom}
     right = {"dom": (me + 1) % ndom}
+    other_core = {"dom": me + 1 - 2 * core}
 
     loads = [
         pltpu.make_async_copy(src, dst, load_sem.at[i])
@@ -253,7 +255,7 @@
     ev_win[0:256] = ev_own
     send(
         ev_win.at[pl.ds(128 * (1 - core), 128)], ev_win.at[pl.ds(256 + 128 * core, 128)], 6,
-        {"dom": me + 1 - 2 * core},
+        other_core,
     )
 
     @pl.when(at_start | at_end)
@@ -287,15 +289,28 @@
     sig = sigmoid(pre)
     slope[256:512] = sig * (1.0 + pre * (1.0 - sig))
 
+    def give(grad, half, half_there, step):
+        half[...] = grad[1 - core].astype(BF16)
+        send(half, half_there, step, other_core)
+
+    def take(grad, half, total, step):
+        wait_for(half, recv_sem.at[step])
+        total[...] = (grad[core] + half[...].astype(F32)).astype(BF16)
+
     sig = sigmoid(agg_one)
+    h_one = (agg_one * sig).astype(BF16)
+    two_f[...] = dot(h_one.T, gz_two).reshape(2, NY, 16, 256)
+    give(two_f, two_give, two_take, 11)
     gs_one = (gh_ref[...] * (sig * (1.0 + agg_one * (1.0 - sig)))).astype(BF16)
     gz_one = dot(adj_t[...], gs_one).astype(BF16)
-    one_src[...] = dot(h_win_t[...], gz_one).astype(BF16).reshape(NZ, 16, 256)
-    h_one = (agg_one * sig).astype(BF16)
-    two_src[...] = dot(h_one.T, gz_two).astype(BF16).reshape(NZ, 16, 256)
-    scatter((one_src, one_dst, my_z, 10, "zc"), (two_src, two_dst, my_yc, 11, "yc"))
+    one_f[...] = dot(h_win_t[...], gz_one).reshape(2, NY, 16, 256)
+    give(one_f, one_give, one_take, 10)
+    take(two_f, two_take, two_src, 11)
+    scatter((two_src, two_dst, my_y, 25, "y"))
     gh_zero = dot(gz_one, w_one_t[...]).astype(BF16)
     g_enc = (gh_zero.astype(F32) * slope[...]).astype(BF16)
+    take(one_f, one_take, one_src, 10)
+    scatter((one_src, one_dst, my_zc, 24, "z"))
     enc_src[...] = dot(ev_win_t[...], g_enc).astype(BF16).reshape(NY, 16, 256)
     scatter((enc_src, enc_dst, my_xc, 12, "xc"))
     z_two[0:256] = dot(h_one, w_two[...]).astype(BF16)
@@ -306,10 +321,10 @@
     arrived(enc_dst, 12, NY - 1)
     enc_y[my_y] = summed(enc_dst)
     spread_out(enc_y, my_y, 13, "y")
-    arrived(one_dst, 10, NZ - 1)
+    arrived(one_dst, 24, NY - 1)
     one_mid[my_y] = summed(one_dst)
     spread_out(one_mid, my_y, 14, "y")
-    arrived(two_dst, 11, NZ - 1)
+    arrived(two_dst, 25, NY - 1)
     two_mid[my_zc] = summed(two_dst)
     spread_out(two_mid, my_zc, 15, "z")
     send(z_two.at[pl.ds(0, 128)], z_two.at[pl.ds(384, 128)], 8, left)
@@ -318,31 +333,41 @@
     enc_z[my_zc] = summed(enc_y)
     spread_out(enc_z, my_zc, 16, "z")
     arrived(one_mid, 14, NY - 1)
-    one_x[rep] = summed(one_mid)
+    one_x[rep] = jnp.sum(one_mid[...].astype(F32), axis=0)
     spread_out(one_x, rep, 17, "x")
     arrived(two_mid, 15, NY - 1)
-    two_x[rep] = summed(two_mid)
+    two_x[rep] = jnp.sum(two_mid[...].astype(F32), axis=0)
     spread_out(two_x, rep, 18, "x")
     wait_for(z_two.at[pl.ds(384, 128)], recv_sem.at[8])
     wait_for(z_two.at[pl.ds(256, 128)], recv_sem.at[9])
     embed[0] = (dot(adj[...], z_two[...]) * inv_deg[...]).astype(BF16)
     arrived(one_x, 17, NX - 1)
-    one_all[my_z] = summed(one_x)
-    spread_out(one_all, my_z, 19, "zc")
+    one_mine = one_all.at[core]
+    one_mine[my_zc] = jnp.sum(one_x[...], axis=0).astype(BF16)
+    spread_out(one_mine, my_zc, 19, "z")
     arrived(two_x, 18, NX - 1)
-    two_all[my_yc] = summed(two_x)
-    spread_out(two_all, my_yc, 20, "yc")
+    two_mine = two_all.at[core]
+    two_mine[my_y] = jnp.sum(two_x[...], axis=0).astype(BF16)
+    spread_out(two_mine, my_y, 20, "y")
     arrived(enc_z, 16, NY - 1)
     enc_all[my_xc] = summed(enc_z)
     spread_out(enc_all, my_xc, 21, "xc")
+    arrived(one_mine, 19, NY - 1)
+    send(one_mine, one_mine, 26, other_core)
+    arrived(two_mine, 20, NY - 1)
+    send(two_mine, two_mine, 27, other_core)
     arrived(enc_all, 21, NY - 1)
-    arrived(one_all, 19, NZ - 1)
-    arrived(two_all, 20, NZ - 1)
+    wait_for(one_all.at[1 - core], recv_sem.at[26])
+    wait_for(two_all.at[1 - core], recv_sem.at[27])
 
     for step, ref in ((0, a_src), (1, ai_src), (13, enc_y), (14, one_mid), (15, two_mid), (16, enc_z)):
         left_all(ref, step, NY - 1)
-    for step, ref in ((2, b_dst), (3, bi_dst), (10, one_src), (11, two_src), (19, one_all), (20, two_all)):
+    for step, ref in ((2, b_dst), (3, bi_dst)):
         left_all(ref, step, NZ - 1)
+    for step, ref in ((24, one_src), (25, two_src), (19, one_mine), (20, two_mine)):
+        left_all(ref, step, NY - 1)
+    for step, ref in ((10, one_give), (11, two_give), (26, one_mine), (27, two_mine)):
+        left_all(ref, step, NY)
     for step, ref in ((12, enc_src), (21, enc_all)):
         left_all(ref, step, NY - 1)
     for step, ref in ((17, one_x), (18, two_x)):
@@ -389,8 +414,8 @@
         out_shape=(
             jax.ShapeDtypeStruct((1, 256, 256), BF16),
             jax.ShapeDtypeStruct((NY, 16, 256), BF16),
-            jax.ShapeDtypeStruct((NZ, 16, 256), BF16),
-            jax.ShapeDtypeStruct((NZ, 16, 256), BF16),
+            jax.ShapeDtypeStruct((2, NY, 16, 256), BF16),
+            jax.ShapeDtypeStruct((2, NY, 16, 256), BF16),
         ),
         in_specs=[hbm] * 6 + [smem] + [hbm] * 2,
         out_specs=(vmem, vmem, vmem, vmem),
@@ -431,14 +456,20 @@
             pieces(NZ, 128, dtype=F32),
             pieces(2, 128, 256),
             pieces(2, 128, 256),
-            pieces(NZ, 16, 256),
-            pieces(NZ, 16, 256),
-            pieces(NY, 16, 256),
-            pieces(NX, 16, 256),
-            pieces(NZ, 16, 256),
-            pieces(NZ, 16, 256),
-            pieces(NY, 16, 256),
-            pieces(NX, 16, 256),
+            pieces(2, NY, 16, 256, dtype=F32),
+            pieces(NY, 16, 256),
+            pieces(NY, 16, 256),
+            pieces(NY, 16, 256),
+            pieces(NY, 16, 256),
+            pieces(NY, 16, 256),
+            pieces(NX, 16, 256, dtype=F32),
+            pieces(2, NY, 16, 256, dtype=F32),
+            pieces(NY, 16, 256),
+            pieces(NY, 16, 256),
+            pieces(NY, 16, 256),
+            pieces(NY, 16, 256),
+            pieces(NY, 16, 256),
+            pieces(NX, 16, 256, dtype=F32),
             pieces(NY, 16, 256),
             pieces(NY, 16, 256),
             pieces(NY, 16, 256),
@@ -447,8 +478,8 @@
             pieces(128, 512),
             pieces(512, 256, dtype=F32),
             pltpu.SemaphoreType.DMA((8,)),
-            pltpu.SemaphoreType.DMA((24,)),
-            pltpu.SemaphoreType.DMA((24,)),
+            pltpu.SemaphoreType.DMA((28,)),
+            pltpu.SemaphoreType.DMA((28,)),
         ],
         compiler_params=pltpu.CompilerParams(
             collective_id=0, has_side_effects=True, vmem_limit_bytes=16 * 1024 * 1024

time: 50.2 us -> 51.9 us (1.034)
  Pallas kernels: 48.7 us -> 50.5 us
    pallas_call x1, Pallas kernels: 47.8 us -> 49.6 us  [body(): pl.pallas_call(functools.partial(step_kernel, scale_loss), out_shape=(jax...]
where the time goes in v11:
time: 51.9 us; the launch traced here: 51.8 us
  Pallas kernels  50.5 us (97%)
  between operations  1.29 us (2%)
    pallas_call x1, Pallas kernels, body(): pl.pallas_call(functools.partial(step_kernel, scale_loss), out_shape=(jax...  49.6 us

profile of v11, /device:TPU:1, one launch (start us, length us, event | category | flops | bytes accessed | tf_op | source)
XLA Modules:
  0.0 51.8 jit_solution(2164383994272073076)
XLA Ops:
  1.3 49.6 %shard_map.120 = (bf16[1,256,256]{2,1,0:T(8,128)(2,1)S(1)}, bf16[8,16,256]{2,1,0:T(8,128)(2,1)S(1)}, bf16[2,8,16,256]{3,2,1,0:T(8,128)(2,1)S(1)}, bf16[2,8,16,256]{3,2,1,0:T(8,128)(2,1)S(1)}) custom-call(bf16[1,256,128]{2,1,0:T(8,128)(2,1)} %events_in.1, s32[1,256]{1,0:T(1,128)} %perm_in.1, bf16[128,256]{1,0:T(8,128)(2,1)} %w_enc_in.1, ...), custom_call_target="tpu_custom_call" | custom-call | tf_op jit(solution)/shard_map/pallas_call | solution.py:412
  50.9 0.9 %shard_map.121 = (bf16[1,256,256]{2,1,0:T(8,128)(2,1)}, f32[128,256]{1,0:T(8,128)}, f32[256,256]{1,0:T(8,128)}, f32[256,256]{1,0:T(8,128)}) custom-call(bf16[1,256,256]{2,1,0:T(8,128)(2,1)S(1)} %get-tuple-element.8.embed, bf16[8,16,256]{2,1,0:T(8,128)(2,1)S(1)} %get-tuple-element.9.enc_all, bf16[2,8,16,256]{3,2,1,0:T(8,128)(2,1)S(1)} %get-tuple-element.10.one_all, ...), custom_call_target="tpu_custom_call" | custom-call | tf_op jit(solution)/shard_map/pallas_call | solution.py:488

commit v12 on v9

--- a/solution.py
+++ b/solution.py
@@ -49,7 +49,7 @@
     ev_win, z_two, gz_ref, gh_ref,
     a_src, a_dst, ai_src, ai_dst, b_src, b_dst, bi_src, bi_dst, edge, edge_i, far_rows, far_ids, qa_src, qa_dst,
     two_src, two_dst, two_mid, two_x, one_src, one_dst, one_mid, one_x,
-    enc_src, enc_dst, enc_y, enc_z, h_win_t, ev_win_t, slope,
+    enc_src, enc_dst, enc_y, enc_z, h_win_t, pre_win,
     load_sem, send_sem, recv_sem,
 ):
     me = lax.axis_index("dom")
@@ -273,19 +273,14 @@
     pre, h_zero = encoded(ev_own)
     z_own = dot(h_zero, w_one[...]).astype(BF16)
     total = dot(adj[:, 0:256], z_own)
-    sig = sigmoid(pre)
-    slope[0:256] = sig * (1.0 + pre * (1.0 - sig))
+    pre_win[0:256] = pre
     h_win_t[:, 0:256] = h_zero.T
-    ev_win_t[:, 0:256] = ev_own.T
     wait_for(ev_win.at[pl.ds(384 - 128 * core, 128)], recv_sem.at[6])
-    ev_side = ev_win[256:512]
-    pre, h_zero = encoded(ev_side)
+    pre, h_zero = encoded(ev_win[256:512])
     z_side = dot(h_zero, w_one[...]).astype(BF16)
     agg_one = (total + dot(adj[:, 256:512], z_side)) * inv_deg[...]
+    pre_win[256:512] = pre
     h_win_t[:, 256:512] = h_zero.T
-    ev_win_t[:, 256:512] = ev_side.T
-    sig = sigmoid(pre)
-    slope[256:512] = sig * (1.0 + pre * (1.0 - sig))
 
     sig = sigmoid(agg_one)
     gs_one = (gh_ref[...] * (sig * (1.0 + agg_one * (1.0 - sig)))).astype(BF16)
@@ -295,8 +290,10 @@
     two_src[...] = dot(h_one.T, gz_two).astype(BF16).reshape(NZ, 16, 256)
     scatter((one_src, one_dst, my_z, 10, "zc"), (two_src, two_dst, my_yc, 11, "yc"))
     gh_zero = dot(gz_one, w_one_t[...]).astype(BF16)
-    g_enc = (gh_zero.astype(F32) * slope[...]).astype(BF16)
-    enc_src[...] = dot(ev_win_t[...], g_enc).astype(BF16).reshape(NY, 16, 256)
+    pre = pre_win[...]
+    sig = sigmoid(pre)
+    g_enc = (gh_zero.astype(F32) * (sig * (1.0 + pre * (1.0 - sig)))).astype(BF16)
+    enc_src[...] = dot(ev_win[...].T, g_enc).astype(BF16).reshape(NY, 16, 256)
     scatter((enc_src, enc_dst, my_xc, 12, "xc"))
     z_two[0:256] = dot(h_one, w_two[...]).astype(BF16)
 
@@ -444,7 +441,6 @@
             pieces(NY, 16, 256),
             pieces(NY, 16, 256),
             pieces(256, 512),
-            pieces(128, 512),
             pieces(512, 256, dtype=F32),
             pltpu.SemaphoreType.DMA((8,)),
             pltpu.SemaphoreType.DMA((24,)),

time: 50.2 us -> 50.2 us (level)
  no operation moved by 1% of the time
where the time goes in v12:
time: 50.2 us; the launch traced here: 50 us
  Pallas kernels  48.7 us (97%)
  between operations  1.29 us (3%)
    pallas_call x1, Pallas kernels, body(): pl.pallas_call(functools.partial(step_kernel, scale_loss), out_shape=(jax...  47.8 us

profile of v12, /device:TPU:1, one launch (start us, length us, event | category | flops | bytes accessed | tf_op | source)
XLA Modules:
  0.0 50.0 jit_solution(16985812920300325182)
XLA Ops:
  1.3 47.8 %shard_map.120 = (bf16[1,256,256]{2,1,0:T(8,128)(2,1)S(1)}, bf16[8,16,256]{2,1,0:T(8,128)(2,1)S(1)}, bf16[16,16,256]{2,1,0:T(8,128)(2,1)S(1)}, bf16[16,16,256]{2,1,0:T(8,128)(2,1)S(1)}) custom-call(bf16[1,256,128]{2,1,0:T(8,128)(2,1)} %events_in.1, s32[1,256]{1,0:T(1,128)} %perm_in.1, bf16[128,256]{1,0:T(8,128)(2,1)} %w_enc_in.1, bf16[256,256]{1,0:T(8,128)(2,1)} %w_one_in.1, ...), custom_call_target="tpu_custom_call" | custom-call | tf_op jit(solution)/shard_map/pallas_call | solution.py:384
  49.1 0.9 %shard_map.121 = (bf16[1,256,256]{2,1,0:T(8,128)(2,1)}, f32[128,256]{1,0:T(8,128)}, f32[256,256]{1,0:T(8,128)}, f32[256,256]{1,0:T(8,128)}) custom-call(bf16[1,256,256]{2,1,0:T(8,128)(2,1)S(1)} %get-tuple-element.8.embed, bf16[8,16,256]{2,1,0:T(8,128)(2,1)S(1)} %get-tuple-element.9.enc_all, bf16[16,16,256]{2,1,0:T(8,128)(2,1)S(1)} %get-tuple-element.10.one_all, ...), custom_call_target="tpu_custom_call" | custom-call | tf_op jit(solution)/shard_map/pallas_call | solution.py:453

commit v13 on v9

--- a/solution.py
+++ b/solution.py
@@ -38,6 +38,10 @@
 
 def one_where(mask):
     return jnp.where(mask, 1.0, 0.0).astype(BF16)
+
+
+def tile(k):
+    return 16 * (k // 2), 128 * (k % 2)
 
 
 def step_kernel(
@@ -48,8 +52,8 @@
     adj_f, adj, adj_t, inv_deg, mid, regroup, spread, finish, w_one_t, w_two_t,
     ev_win, z_two, gz_ref, gh_ref,
     a_src, a_dst, ai_src, ai_dst, b_src, b_dst, bi_src, bi_dst, edge, edge_i, far_rows, far_ids, qa_src, qa_dst,
-    two_src, two_dst, two_mid, two_x, one_src, one_dst, one_mid, one_x,
-    enc_src, enc_dst, enc_y, enc_z, h_win_t, ev_win_t, slope,
+    two_src, two_dst, two_mid, two_x, one_src, one_dst, one_ay, one_az, one_by, one_bz,
+    enc_src, enc_dst, enc_mid, enc_x, h_win_t, ev_win_t, slope,
     load_sem, send_sem, recv_sem,
 ):
     me = lax.axis_index("dom")
@@ -288,64 +292,75 @@
     slope[256:512] = sig * (1.0 + pre * (1.0 - sig))
 
     sig = sigmoid(agg_one)
+    h_one = (agg_one * sig).astype(BF16)
+    two_src[...] = dot(h_one.T, gz_two).astype(BF16).reshape(NZ, 16, 256)
+    scatter((two_src, two_dst, my_yc, 11, "yc"))
     gs_one = (gh_ref[...] * (sig * (1.0 + agg_one * (1.0 - sig)))).astype(BF16)
     gz_one = dot(adj_t[...], gs_one).astype(BF16)
-    one_src[...] = dot(h_win_t[...], gz_one).astype(BF16).reshape(NZ, 16, 256)
-    h_one = (agg_one * sig).astype(BF16)
-    two_src[...] = dot(h_one.T, gz_two).astype(BF16).reshape(NZ, 16, 256)
-    scatter((one_src, one_dst, my_z, 10, "zc"), (two_src, two_dst, my_yc, 11, "yc"))
+    one_src[...] = dot(h_win_t[...], gz_one).astype(BF16).reshape(NY, 32, 256)
+    scatter((one_src, one_dst, my_xc, 10, "xc"))
     gh_zero = dot(gz_one, w_one_t[...]).astype(BF16)
     g_enc = (gh_zero.astype(F32) * slope[...]).astype(BF16)
-    enc_src[...] = dot(ev_win_t[...], g_enc).astype(BF16).reshape(NY, 16, 256)
-    scatter((enc_src, enc_dst, my_xc, 12, "xc"))
+    grad = dot(ev_win_t[...], g_enc).astype(BF16)
+    for k in range(NZ):
+        r, c = tile(k)
+        enc_src[k] = grad[r : r + 16, c : c + 128]
+    scatter((enc_src, enc_dst, my_z, 12, "zc"))
     z_two[0:256] = dot(h_one, w_two[...]).astype(BF16)
 
     def summed(ref):
         return jnp.sum(ref[...].astype(F32), axis=0).astype(BF16)
 
-    arrived(enc_dst, 12, NY - 1)
-    enc_y[my_y] = summed(enc_dst)
-    spread_out(enc_y, my_y, 13, "y")
-    arrived(one_dst, 10, NZ - 1)
-    one_mid[my_y] = summed(one_dst)
-    spread_out(one_mid, my_y, 14, "y")
+    arrived(one_dst, 10, NY - 1)
+    total = summed(one_dst)
+    one_ay[my_y] = total[0:16]
+    one_bz[my_zc] = total[16:32]
+    spread_out(one_ay, my_y, 14, "y")
+    spread_out(one_bz, my_zc, 24, "z")
     arrived(two_dst, 11, NZ - 1)
     two_mid[my_zc] = summed(two_dst)
     spread_out(two_mid, my_zc, 15, "z")
+    arrived(enc_dst, 12, NZ - 1)
+    enc_mid[my_y] = summed(enc_dst)
+    spread_out(enc_mid, my_y, 13, "y")
     send(z_two.at[pl.ds(0, 128)], z_two.at[pl.ds(384, 128)], 8, left)
     send(z_two.at[pl.ds(128, 128)], z_two.at[pl.ds(256, 128)], 9, right)
-    arrived(enc_y, 13, NY - 1)
-    enc_z[my_zc] = summed(enc_y)
-    spread_out(enc_z, my_zc, 16, "z")
-    arrived(one_mid, 14, NY - 1)
-    one_x[rep] = summed(one_mid)
-    spread_out(one_x, rep, 17, "x")
+    arrived(one_ay, 14, NY - 1)
+    one_az[my_zc] = summed(one_ay)
+    spread_out(one_az, my_zc, 17, "z")
+    arrived(one_bz, 24, NY - 1)
+    one_by[my_y] = summed(one_bz)
+    spread_out(one_by, my_y, 25, "y")
     arrived(two_mid, 15, NY - 1)
     two_x[rep] = summed(two_mid)
     spread_out(two_x, rep, 18, "x")
+    arrived(enc_mid, 13, NY - 1)
+    enc_x[rep] = summed(enc_mid)
+    spread_out(enc_x, rep, 16, "x")
     wait_for(z_two.at[pl.ds(384, 128)], recv_sem.at[8])
     wait_for(z_two.at[pl.ds(256, 128)], recv_sem.at[9])
     embed[0] = (dot(adj[...], z_two[...]) * inv_deg[...]).astype(BF16)
-    arrived(one_x, 17, NX - 1)
-    one_all[my_z] = summed(one_x)
-    spread_out(one_all, my_z, 19, "zc")
     arrived(two_x, 18, NX - 1)
     two_all[my_yc] = summed(two_x)
     spread_out(two_all, my_yc, 20, "yc")
-    arrived(enc_z, 16, NY - 1)
-    enc_all[my_xc] = summed(enc_z)
-    spread_out(enc_all, my_xc, 21, "xc")
-    arrived(enc_all, 21, NY - 1)
-    arrived(one_all, 19, NZ - 1)
+    arrived(enc_x, 16, NX - 1)
+    enc_all[my_z] = summed(enc_x)
+    spread_out(enc_all, my_z, 21, "zc")
+    arrived(one_az, 17, NY - 1)
+    arrived(one_by, 25, NY - 1)
+    one_all[my_xc] = jnp.concatenate([summed(one_az), summed(one_by)], axis=0)
+    spread_out(one_all, my_xc, 19, "xc")
+    arrived(enc_all, 21, NZ - 1)
+    arrived(one_all, 19, NY - 1)
     arrived(two_all, 20, NZ - 1)
 
-    for step, ref in ((0, a_src), (1, ai_src), (13, enc_y), (14, one_mid), (15, two_mid), (16, enc_z)):
+    for step, ref in ((0, a_src), (1, ai_src), (13, enc_mid), (14, one_ay), (15, two_mid), (24, one_bz)):
         left_all(ref, step, NY - 1)
-    for step, ref in ((2, b_dst), (3, bi_dst), (10, one_src), (11, two_src), (19, one_all), (20, two_all)):
+    for step, ref in ((10, one_src), (17, one_az), (25, one_by), (19, one_all)):
+        left_all(ref, step, NY - 1)
+    for step, ref in ((2, b_dst), (3, bi_dst), (12, enc_src), (11, two_src), (21, enc_all), (20, two_all)):
         left_all(ref, step, NZ - 1)
-    for step, ref in ((12, enc_src), (21, enc_all)):
-        left_all(ref, step, NY - 1)
-    for step, ref in ((17, one_x), (18, two_x)):
+    for step, ref in ((16, enc_x), (18, two_x)):
         left_all(ref, step, NX - 1)
     for step, ref in ((4, qa_src), (5, qa_src)):
         left_all(ref, step, 1)
@@ -360,12 +375,15 @@
 ):
     stores = [pltpu.make_async_copy(embed, embed_out, sem.at[0])]
     stores[0].start()
-    for i, (src, wide, out) in enumerate(
-        ((enc_all, enc, grad_enc), (one_all, one, grad_one), (two_all, two, grad_two))
-    ):
+    for i, (src, wide, out) in enumerate(((one_all, one, grad_one), (two_all, two, grad_two))):
         wide[...] = src[...].astype(F32).reshape(wide.shape)
         stores.append(pltpu.make_async_copy(wide, out, sem.at[i + 1]))
         stores[-1].start()
+    for k in range(NZ):
+        r, c = tile(k)
+        enc[r : r + 16, c : c + 128] = enc_all[k].astype(F32)
+    stores.append(pltpu.make_async_copy(enc, grad_enc, sem.at[3]))
+    stores[3].start()
     for store in stores:
         store.wait()
 
@@ -388,8 +406,8 @@
         functools.partial(step_kernel, scale_loss),
         out_shape=(
             jax.ShapeDtypeStruct((1, 256, 256), BF16),
-            jax.ShapeDtypeStruct((NY, 16, 256), BF16),
-            jax.ShapeDtypeStruct((NZ, 16, 256), BF16),
+            jax.ShapeDtypeStruct((NZ, 16, 128), BF16),
+            jax.ShapeDtypeStruct((NY, 32, 256), BF16),
             jax.ShapeDtypeStruct((NZ, 16, 256), BF16),
         ),
         in_specs=[hbm] * 6 + [smem] + [hbm] * 2,
@@ -435,20 +453,22 @@
             pieces(NZ, 16, 256),
             pieces(NY, 16, 256),
             pieces(NX, 16, 256),
-            pieces(NZ, 16, 256),
-            pieces(NZ, 16, 256),
-            pieces(NY, 16, 256),
-            pieces(NX, 16, 256),
+            pieces(NY, 32, 256),
+            pieces(NY, 32, 256),
             pieces(NY, 16, 256),
             pieces(NY, 16, 256),
             pieces(NY, 16, 256),
             pieces(NY, 16, 256),
+            pieces(NZ, 16, 128),
+            pieces(NZ, 16, 128),
+            pieces(NY, 16, 128),
+            pieces(NX, 16, 128),
             pieces(256, 512),
             pieces(128, 512),
             pieces(512, 256, dtype=F32),
             pltpu.SemaphoreType.DMA((8,)),
-            pltpu.SemaphoreType.DMA((24,)),
-            pltpu.SemaphoreType.DMA((24,)),
+            pltpu.SemaphoreType.DMA((26,)),
+            pltpu.SemaphoreType.DMA((26,)),
         ],
         compiler_params=pltpu.CompilerParams(
             collective_id=0, has_side_effects=True, vmem_limit_bytes=16 * 1024 * 1024

time: 50.2 us -> 49.9 us (level)
  no operation moved by 1% of the time
where the time goes in v13:
time: 49.9 us; the launch traced here: 49.7 us
  Pallas kernels  48.5 us (97%)
  between operations  1.29 us (3%)
    pallas_call x1, Pallas kernels, body(): pl.pallas_call(functools.partial(step_kernel, scale_loss), out_shape=(jax...  47.5 us

profile of v13, /device:TPU:1, one launch (start us, length us, event | category | flops | bytes accessed | tf_op | source)
XLA Modules:
  0.0 49.7 jit_solution(11147354939571337845)
XLA Ops:
  1.3 47.5 %shard_map.120 = (bf16[1,256,256]{2,1,0:T(8,128)(2,1)S(1)}, bf16[16,16,128]{2,1,0:T(8,128)(2,1)S(1)}, bf16[8,32,256]{2,1,0:T(8,128)(2,1)S(1)}, bf16[16,16,256]{2,1,0:T(8,128)(2,1)S(1)}) custom-call(bf16[1,256,128]{2,1,0:T(8,128)(2,1)} %events_in.1, s32[1,256]{1,0:T(1,128)} %perm_in.1, bf16[128,256]{1,0:T(8,128)(2,1)} %w_enc_in.1, bf16[256,256]{1,0:T(8,128)(2,1)} %w_one_in.1, ...), custom_call_target="tpu_custom_call" | custom-call | tf_op jit(solution)/shard_map/pallas_call | solution.py:405
  48.8 0.9 %shard_map.121 = (bf16[1,256,256]{2,1,0:T(8,128)(2,1)}, f32[128,256]{1,0:T(8,128)}, f32[256,256]{1,0:T(8,128)}, f32[256,256]{1,0:T(8,128)}) custom-call(bf16[1,256,256]{2,1,0:T(8,128)(2,1)S(1)} %get-tuple-element.8.embed, bf16[16,16,128]{2,1,0:T(8,128)(2,1)S(1)} %get-tuple-element.9.enc_all, bf16[8,32,256]{2,1,0:T(8,128)(2,1)S(1)} %get-tuple-element.10.one_all, ...), custom_call_target="tpu_custom_call" | custom-call | tf_op jit(solution)/shard_map/pallas_call | solution.py:477
